TPU v7x, 256 devices: a whole 4x4x8 slice. The times are simulated.
256 devices in a mesh: section: 8 (over x_lo, y), shard: 32 (over z, x_hi, core).
Axes of the slice: x: 4 (x_hi: 2, x_lo: 2; x = x_hi * 2 + x_lo), y: 4, z: 8, core: 2. Of those that a mesh axis runs over, the one named last changes fastest.
Arguments:
- states: bfloat16 [2048, 8192], P('section', 'shard'), may hold values from -6 to 6
- lengths: int32 [8], replicated, may hold values from 64 to 256, as said below
- gate_weight: bfloat16 [8192, 14336], P(('section', 'shard')), may hold values from -0.0625 to 0.0625
- up_weight: bfloat16 [8192, 14336], P(('section', 'shard')), may hold values from -0.0625 to 0.0625
- upstream: bfloat16 [2048, 14336], P('section', 'shard'), may hold values from -6 to 6
Outputs:
- hidden: bfloat16 [2048, 14336], P('section', 'shard')
- new_gate: bfloat16 [8192, 14336], P('section', 'shard')
- new_up: bfloat16 [8192, 14336], P('section', 'shard')
Inputs may be any that keep to these rules, and one draw needn't show every extreme that they name: `lengths`: some rollout has length exactly 256.
All inputs are finite; a program needn't handle non-finite values.
Results may differ from a plain program's by a relative error of at most 0.015.
Values may be sent and summed in bfloat16 or wider, within the bound.
A program may use at most 128 MiB of HBM per device.

v0:
```python
import jax
import jax.numpy as jnp
from jax import lax
from jax.sharding import PartitionSpec as P


def shards(states, lengths, gate_weight, up_weight, upstream):
    rows_all = lax.all_gather(states, "shard", axis=1, tiled=True)
    gate_mid, up_mid = (
        lax.all_to_all(gate_weight, "shard", split_axis=1, concat_axis=0, tiled=True),
        lax.all_to_all(up_weight, "shard", split_axis=1, concat_axis=0, tiled=True),
    )
    span = rows_all.shape[0]
    width = gate_mid.shape[1]
    columns = rows_all
    gate = jnp.dot(
        columns,
        lax.all_gather(gate_mid, "section", axis=0, tiled=True),
        preferred_element_type=jnp.float32,
    )
    upval = jnp.dot(
        columns,
        lax.all_gather(up_mid, "section", axis=0, tiled=True),
        preferred_element_type=jnp.float32,
    )
    sigma = jax.nn.sigmoid(gate)
    active = gate * sigma
    hidden = (active * upval).astype(jnp.bfloat16)
    section_id = lax.axis_index("section")
    sections = lax.axis_size("section")
    own_length = jnp.sum(jnp.where(jnp.arange(sections) == section_id, lengths, 0))
    live = (jnp.arange(span) < own_length)[:, None]
    grad_h = jnp.where(live, upstream.astype(jnp.float32), 0.0)
    d_gate = grad_h * upval * sigma * (1.0 + gate * (1.0 - sigma))
    d_up = grad_h * active
    stacked = jnp.concatenate([d_gate, d_up], 1).astype(jnp.bfloat16)
    columns = rows_all
    total = lax.psum_scatter(
        jnp.dot(columns.T, stacked, preferred_element_type=jnp.float32).astype(jnp.bfloat16),
        "section",
        scatter_dimension=0,
        tiled=True,
    ).astype(jnp.float32)
    scale = 0.5 / jnp.sum(lengths).astype(jnp.float32)
    new_gate = (gate_mid.astype(jnp.float32) - scale * total[:, :width]).astype(jnp.bfloat16)
    new_up = (up_mid.astype(jnp.float32) - scale * total[:, width:]).astype(jnp.bfloat16)
    return (hidden, new_gate, new_up)


def solution(mesh):
    in_specs = (
        P("section", "shard"),
        P(),
        P(("section", "shard"), None),
        P(("section", "shard"), None),
        P("section", "shard"),
    )
    out_specs = (P("section", "shard"), P("section", "shard"), P("section", "shard"))
    return jax.shard_map(shards, mesh=mesh, in_specs=in_specs, out_specs=out_specs, check_vma=False)
```

profile of v0, /device:TPU:36, one launch (start us, length us, event | category | flops | bytes accessed | tf_op | source)
XLA Modules:
  0.0 482.2 jit_solution(570348037665714542)
XLA Ops:
  7.2 0.0 copy-start.3
  7.2 0.0 all-gather.4.cloned.1.call-start
  7.2 0.7 all-gather.4.cloned.1.call-update
  7.9 0.0 all-gather.8.cloned.1.call-start
  8.0 2.4 all_to_all.32
  10.4 0.6 copy.11
  10.9 41.9 %all_to_all.38 = bf16[32,32,448]{2,0,1:T(8,128)(2,1)} all-to-all(bf16[32,32,448]{2,0,1:T(8,128)(2,1)S(1)} %copy.11), channel_id=1, replica_groups=mesh['section'=8,'shard'=32] {'shard'}, dimensions={1} | all-to-all | bytes 1835008 | tf_op jit(solution)/shard_map/all_to_all | solution.py:11
  52.9 0.0 copy-start.4
  52.9 0.0 all-gather.8.cloned.1.call-update
  52.9 0.0 all-gather.6.cloned.1.call-start
  52.9 0.0 copy-done.3
  52.9 1.2 all_to_all.28
  54.2 0.6 copy.10
  54.8 36.8 %all_to_all.39 = bf16[32,32,448]{2,0,1:T(8,128)(2,1)} all-to-all(bf16[32,32,448]{2,0,1:T(8,128)(2,1)S(1)} %copy.10), channel_id=1, replica_groups=mesh['section'=8,'shard'=32] {'shard'}, dimensions={1} | all-to-all | bytes 1835008 | tf_op jit(solution)/shard_map/all_to_all | solution.py:10
  91.6 0.0 all-gather.6.cloned.1.call-update
  91.6 0.2 reduce-scatter.2.cloned.1.call-start
  91.9 0.0 copy-done.4
  91.9 0.6 fusion.10
  92.5 0.6 iota_compare_fusion
  93.2 0.0 copy-start.5
  93.2 17.6 %all-gather.4.cloned.1.call-done = bf16[256,8192]{1,0:T(8,128)(2,1)} async-done(((bf16[256,256]{1,0:T(8,128)(2,1)}), bf16[256,8192]{1,0:T(8,128)(2,1)}) %all-gather.4.cloned.1.call-update) | async-done | bytes 4194320 | tf_op jit(solution)/shard_map/all_gather | solution.py:8
  110.8 96.2 %all-gather.8.cloned.1.call-done = bf16[8192,448]{1,0:T(8,128)(2,1)} async-done(((bf16[1024,448]{1,0:T(8,128)(2,1)}), bf16[8192,448]{1,0:T(8,128)(2,1)}) %all-gather.8.cloned.1.call-update) | async-done | bytes 7340048 | tf_op jit(solution)/shard_map/all_gather | solution.py:23
  207.1 7.8 %fusion.11 = f32[256,448]{0,1:T(8,128)S(1)} fusion(bf16[256,8192]{1,0:T(8,128)(2,1)} %all-gather.4.cloned.1.call-done, bf16[8192,448]{1,0:T(8,128)(2,1)} %all-gather.8.cloned.1.call-done), kind=kOutput, calls=%fused_computation.21 | convolution fusion | flops 1879048192 | bytes 11993088 | tf_op jit(solution)/shard_map/dot_general | solution.py:21
  214.9 87.3 %all-gather.6.cloned.1.call-done = bf16[8192,448]{1,0:T(8,128)(2,1)} async-done(((bf16[1024,448]{1,0:T(8,128)(2,1)}), bf16[8192,448]{1,0:T(8,128)(2,1)}) %all-gather.6.cloned.1.call-update) | async-done | bytes 7340048 | tf_op jit(solution)/shard_map/all_gather | solution.py:18
  302.2 0.0 copy-done.5
  302.2 0.0 copy-start.2
  302.2 8.8 %multiply_convert_fusion.1 = (bf16[256,448]{0,1:T(8,128)(2,1)S(1)}, bf16[256,448]{0,1:T(8,128)(2,1)}, bf16[256,448]{0,1:T(8,128)(2,1)S(1)}) fusion(f32[256,448]{0,1:T(8,128)S(1)} %fusion.11, bf16[256,448]{0,1:T(8,128)(2,1)S(1)} %copy-done.5, pred[256]{0:T(512)(128)(4,1)S(1)} %iota_compare_fusion, bf16[256,8192]{1,0:T(8,128)(2,1)} %all-gather.4.cloned.1.call-done, ...), kind=kOutput, calls=%fused_computation.11 | convolution fusion | flops 1880997888 | bytes 12910848 | tf_op jit(solution)/shard_map/dot_general | solution.py:16
  311.0 0.0 copy-done.2
  311.0 7.3 %convert_bitcast_fusion = bf16[8192,896]{0,1:T(8,128)(2,1)} fusion(bf16[256,8192]{1,0:T(8,128)(2,1)S(1)} %copy-done.2, bf16[256,448]{0,1:T(8,128)(2,1)S(1)} %get-tuple-element.9, bf16[256,448]{0,1:T(8,128)(2,1)S(1)} %get-tuple-element.7), kind=kOutput, calls=%fused_computation | convolution fusion | flops 3766353920 | bytes 19333120 | tf_op jit(solution)/shard_map/dot_general | solution.py:39
  318.2 0.0 copy-start
  318.3 0.0 copy-start.1
  318.3 0.0 reduce-scatter.2.cloned.1.call-update
  319.1 0.4 copy-done
  319.5 0.5 copy.13
  320.0 0.0 copy-done.1
  320.0 0.5 copy.12
  320.5 151.3 %reduce-scatter.2.cloned.1.call-done = bf16[1024,896]{0,1:T(8,128)(2,1)} async-done(((bf16[8192,896]{0,1:T(8,128)(2,1)}), bf16[1024,896]{0,1:T(8,128)(2,1)}) %reduce-scatter.2.cloned.1.call-update) | async-done | bytes 1835024 | tf_op jit(solution)/shard_map/reduce_scatter | solution.py:38
  471.9 1.9 convert_element_type.37
  473.8 1.9 fusion.1
Async XLA Ops:
  7.2 45.8 %copy-start.3 = (bf16[32,14336]{1,0:T(8,128)(2,1)S(1)}, bf16[32,14336]{1,0:T(8,128)(2,1)}, u32[]{:S(2)}) copy-start(bf16[32,14336]{1,0:T(8,128)(2,1)} %param.7) | copy-start | bytes 2752516
  7.2 103.6 %all-gather.4.cloned.1.call-start = ((), (), s32[]{:S(2)}) async-start(), calls=%async_computation.3 | async-start | bytes 4325376 | tf_op jit(solution)/shard_map/all_gather | solution.py:8
  7.9 199.2 %all-gather.8.cloned.1.call-start = ((), (), s32[]{:S(2)}) async-start(), calls=%async_computation.5 | async-start | bytes 9437184 | tf_op jit(solution)/shard_map/all_gather | solution.py:23
  52.9 39.0 %copy-start.4 = (s32[8]{0:T(128)S(1)}, s32[8]{0:T(128)}, u32[]{:S(2)}) copy-start(s32[8]{0:T(128)} %param.6) | copy-start | bytes 100
  52.9 249.3 %all-gather.6.cloned.1.call-start = ((), (), s32[]{:S(2)}) async-start(), calls=%async_computation.4 | async-start | bytes 9437184 | tf_op jit(solution)/shard_map/all_gather | solution.py:18
  91.6 380.2 %reduce-scatter.2.cloned.1.call-start = ((), (), s32[]{:S(2)}) async-start(), calls=%async_computation.6 | async-start | bytes 16515072 | tf_op jit(solution)/shard_map/reduce_scatter | solution.py:38
  93.2 209.0 %copy-start.5 = (bf16[256,448]{0,1:T(8,128)(2,1)S(1)}, bf16[256,448]{0,1:T(8,128)(2,1)}, u32[]{:S(2)}) copy-start(bf16[256,448]{0,1:T(8,128)(2,1)} %param.9) | copy-start | bytes 688132
  302.2 8.8 %copy-start.2 = (bf16[256,8192]{1,0:T(8,128)(2,1)S(1)}, bf16[256,8192]{1,0:T(8,128)(2,1)}, u32[]{:S(2)}) copy-start(bf16[256,8192]{1,0:T(8,128)(2,1)} %all-gather.4.cloned.1.call-done) | copy-start | bytes 12582916
  318.2 1.2 copy-start
  318.3 1.7 copy-start.1
Sparse Core Ops, SparseCore 0:
  10.6 100.2 all-gather.3
  112.6 94.4 all-gather.7
  208.9 93.2 all-gather.5
  318.4 153.4 reduce-scatter.1
where the time goes:
time: 484 us; the launch traced here: 482 us
  waiting for transfers between devices  353 us (73%)
  blocking collectives  78.7 us (16%)
  matrix products  23.9 us (5%)
  between operations  14.7 us (3%)
  local copies, waits for them, and re-layouts  6.2 us (1%)
  other arithmetic  5.09 us (1%)
    reduce_scatter x1, waiting for transfers between devices, shards(): lax.psum_scatter(jnp.dot(columns.T, stacked, preferred_element_type=jnp.f...  151 us
    all_gather x1, waiting for transfers between devices, shards(): lax.all_gather(up_mid, 'section', axis=0, tiled=True)  96.2 us
    all_gather x1, waiting for transfers between devices, shards(): lax.all_gather(gate_mid, 'section', axis=0, tiled=True)  87.3 us
    all_to_all x1, blocking collectives, shards(): lax.all_to_all(up_weight, 'shard', split_axis=1, concat_axis=0, tiled=True)  41.9 us
    all_to_all x1, blocking collectives, shards(): lax.all_to_all(gate_weight, 'shard', split_axis=1, concat_axis=0, tiled=T...  36.8 us
    all_gather x1, waiting for transfers between devices, shards(): rows_all = lax.all_gather(states, 'shard', axis=1, tiled=True)  17.6 us
  transfers between devices with their start and end apart: 4, of which 4 were waited for; matrix products, arithmetic and copies ran while one was open for 2% of the time, Pallas kernels for 0%

commit v1 on v0

v1 whole, which is shorter than its diff:
```python
import jax
import jax.numpy as jnp
from jax import lax
from jax.sharding import PartitionSpec as P


def shards(states, lengths, gate_weight, up_weight, upstream):
    sections = lax.axis_size("section")
    shard_n = lax.axis_size("shard")
    section_id = lax.axis_index("section")
    span, cols = states.shape
    quarter = shard_n // sections
    perm = []
    for s in range(sections):
        for j in range(shard_n):
            perm.append((s * shard_n + j, (j // quarter) * shard_n + s * quarter + j % quarter))
    moved = lax.ppermute(states, ("section", "shard"), perm)
    blocks = lax.all_gather(moved, "shard", axis=0, tiled=False)
    rows = blocks.reshape(sections, quarter, span, cols).transpose(0, 2, 1, 3)
    rows = rows.reshape(sections * span, quarter * cols)

    depth, units = gate_weight.shape
    width = units // shard_n
    both = jnp.concatenate(
        [gate_weight.reshape(depth, shard_n, width), up_weight.reshape(depth, shard_n, width)], 2
    )
    both = lax.all_to_all(both, "shard", split_axis=1, concat_axis=0, tiled=True)
    both = both.reshape(depth * shard_n, 2 * width)

    partial = jnp.dot(rows, both, preferred_element_type=jnp.float32).astype(jnp.bfloat16)
    pair = lax.psum_scatter(partial, "section", scatter_dimension=0, tiled=True).astype(jnp.float32)
    gate, upval = pair[:, :width], pair[:, width:]
    sigma = jax.nn.sigmoid(gate)
    active = gate * sigma
    hidden = (active * upval).astype(jnp.bfloat16)
    own_length = jnp.sum(jnp.where(jnp.arange(sections) == section_id, lengths, 0))
    live = (jnp.arange(span) < own_length)[:, None]
    grad_h = jnp.where(live, upstream.astype(jnp.float32), 0.0)
    d_gate = grad_h * upval * sigma * (1.0 + gate * (1.0 - sigma))
    d_up = grad_h * active
    stacked = jnp.concatenate([d_gate, d_up], 1).astype(jnp.bfloat16)
    grads = lax.all_gather(stacked, "section", axis=0, tiled=True)
    total = jnp.dot(rows.T, grads, preferred_element_type=jnp.float32)
    scale = 0.5 / jnp.sum(lengths).astype(jnp.float32)
    new = (both.astype(jnp.float32) - scale * total).astype(jnp.bfloat16)
    return (hidden, new[:, :width], new[:, width:])


def solution(mesh):
    in_specs = (
        P("section", "shard"),
        P(),
        P(("section", "shard"), None),
        P(("section", "shard"), None),
        P("section", "shard"),
    )
    out_specs = (P("section", "shard"), P("section", "shard"), P("section", "shard"))
    return jax.shard_map(shards, mesh=mesh, in_specs=in_specs, out_specs=out_specs, check_vma=False)
```

time: 484 us -> 277 us (0.57)
  waiting for transfers between devices: 353 us -> 188 us
  blocking collectives: 78.7 us -> 0 us
  starting transfers between devices: 0.34 us -> 22.4 us
  local copies, waits for them, and re-layouts: 6.2 us -> 25.8 us
  matrix products: 23.9 us -> 15.8 us
    reduce_scatter x1, waiting for transfers between devices: 151 us -> 48.8 us  [shards(): lax.psum_scatter(partial, 'section', scatter_dimension=0, tiled=True)]
    all_to_all x2 -> x0, blocking collectives: 78.7 us -> none  [the longest x1 41.9 us: shards(): lax.all_to_all(up_weight, 'shard', split_axis=1, concat_axis=0, tiled=True)]
    all_gather x3 -> x2, waiting for transfers between devices: 201 us -> 130 us  [the longest x1 75.4 us: shards(): blocks = lax.all_gather(moved, 'shard', axis=0, tiled=False)]
    all_to_all x0 -> x1, starting transfers between devices: none -> 19.1 us  [shards(): lax.all_to_all(both, 'shard', split_axis=1, concat_axis=0, tiled=True)]
    reshape x0 -> x4, local copies, waits for them, and re-layouts: none -> 15.9 us  [the longest x1 7.89 us: shards(): rows = blocks.reshape(sections, quarter, span, cols).transpose(0, 2, 1, 3)]
    ppermute x0 -> x1, waiting for transfers between devices: none -> 8.7 us  [shards(): moved = lax.ppermute(states, ('section', 'shard'), perm)]
    dot_general x3 -> x2, matrix products: 23.9 us -> 15.8 us  [the longest x1 8 us: shards(): jnp.dot(rows, both, preferred_element_type=jnp.float32).astype(jnp.bfloat16)]
    unnamed x12 -> x7, local copies, waits for them, and re-layouts: 0.4 us -> 6.67 us
  transfers between devices with their start and end apart: 4 -> 5, of which waited for: 4 -> 4; matrix products, arithmetic and copies ran while one was open for 2% -> 10% of each run, Pallas kernels for 0% -> 0%
where the time goes in v1:
time: 277 us; the launch traced here: 272 us
  waiting for transfers between devices  188 us (68%)
  local copies, waits for them, and re-layouts  25.8 us (9%)
  starting transfers between devices  22.4 us (8%)
  matrix products  15.8 us (6%)
  between operations  14.5 us (5%)
  other arithmetic  5.92 us (2%)
    all_gather x1, waiting for transfers between devices, shards(): blocks = lax.all_gather(moved, 'shard', axis=0, tiled=False)  75.4 us
    all_gather x1, waiting for transfers between devices, shards(): grads = lax.all_gather(stacked, 'section', axis=0, tiled=True)  54.5 us
    reduce_scatter x1, waiting for transfers between devices, shards(): lax.psum_scatter(partial, 'section', scatter_dimension=0, tiled=True)  48.8 us
    all_to_all x1, starting transfers between devices, shards(): lax.all_to_all(both, 'shard', split_axis=1, concat_axis=0, tiled=True)  19.1 us
    ppermute x1, waiting for transfers between devices, shards(): moved = lax.ppermute(states, ('section', 'shard'), perm)  8.7 us
    dot_general x1, matrix products, shards(): jnp.dot(rows, both, preferred_element_type=jnp.float32).astype(jnp.bfloat16)  8 us
    reshape x1, local copies, waits for them, and re-layouts, shards(): rows = blocks.reshape(sections, quarter, span, cols).transpose(0, 2, 1, 3)  7.89 us
    dot_general x1, matrix products, shards(): total = jnp.dot(rows.T, grads, preferred_element_type=jnp.float32)  7.8 us
  transfers between devices with their start and end apart: 5, of which 4 were waited for; matrix products, arithmetic and copies ran while one was open for 10% of the time, Pallas kernels for 0%

profile of v1, /device:TPU:36, one launch (start us, length us, event | category | flops | bytes accessed | tf_op | source)
XLA Modules:
  0.0 272.0 jit_solution(14478304347883859163)
XLA Ops:
  7.2 0.0 all-gather.6.cloned.1.call-start
  7.2 3.0 %collective-permute-start = (bf16[256,256]{1,0:T(8,128)(2,1)}, bf16[256,256]{1,0:T(8,128)(2,1)S(1)}, u32[]{:S(2)}, u32[]{:S(2)}) collective-permute-start(bf16[256,256]{1,0:T(8,128)(2,1)} %param.5), channel_id=1, source_target_pairs={{0,0},{1,1},{2,2},{3,3},{4,32},{5,33},{6,34},{7,35},{8,64},{9,65},... | collective-permute-start | bytes 393224 | tf_op jit(solution)/shard_map/ppermute | solution.py:17
  10.2 8.7 %collective-permute-done = bf16[256,256]{1,0:T(8,128)(2,1)S(1)} collective-permute-done((bf16[256,256]{1,0:T(8,128)(2,1)}, bf16[256,256]{1,0:T(8,128)(2,1)S(1)}, u32[]{:S(2)}, u32[]{:S(2)}) %collective-permute-start) | collective-permute-done | bytes 131104 | tf_op jit(solution)/shard_map/ppermute | solution.py:17
  18.9 0.0 copy-start.1
  18.9 0.7 copy-done.1
  19.6 0.0 all-gather.6.cloned.1.call-update
  19.6 2.4 reshape.27
  22.0 3.1 %reshape.26 = bf16[32,32,448]{2,1,0:T(8,128)(2,1)} reshape(bf16[32,14336]{1,0:T(8,128)(2,1)} %param.7) | data formatting | bytes 1835008 | tf_op jit(solution)/shard_map/reshape | solution.py:25
  25.1 1.8 pad_maximum_fusion
  26.9 1.8 copy.15
  28.8 19.1 %all-to-all-start = ((bf16[32,32,896]{2,0,1:T(8,128)(2,1)}), bf16[32,32,896]{2,0,1:T(8,128)(2,1)S(1)}, u32[]{:S(2)}, u32[]{:S(2)}) async-start(bf16[32,32,896]{2,0,1:T(8,128)(2,1)} %copy.15), calls=%async_computation | async-start | bytes 3670016 | tf_op jit(solution)/shard_map/all_to_all | solution.py:27
  47.9 0.0 reduce-scatter.2.cloned.1.call-start
  47.9 75.4 %all-gather.6.cloned.1.call-done = bf16[8192,256]{1,0:T(8,128)(2,1)} async-done(((bf16[256,256]{1,0:T(8,128)(2,1)}), bf16[8192,256]{1,0:T(8,128)(2,1)}) %all-gather.6.cloned.1.call-update) | async-done | bytes 4194320 | tf_op jit(solution)/shard_map/all_gather | solution.py:18
  123.3 7.9 %copy.16 = bf16[8,4,256,256]{2,0,3,1:T(8,128)(2,1)} copy(bf16[8,4,256,256]{3,2,1,0:T(8,128)(2,1)} %bitcast.27) | data formatting | bytes 8388608 | tf_op jit(solution)/shard_map/reshape | solution.py:19
  131.2 5.6 %copy.18 = bf16[128,8,8,256]{3,1,2,0:T(8,128)(2,1)} copy(bf16[128,8,8,256]{3,2,1,0:T(8,128)(2,1)} %bitcast.22) | data formatting | bytes 8388608
  136.8 0.0 all-to-all-done
  136.8 8.0 %convert_bitcast_fusion = bf16[2048,896]{0,1:T(8,128)(2,1)} fusion(bf16[1024,896]{1,0:T(8,128)(2,1)S(1)} %bitcast.23, bf16[2048,1024]{0,1:T(8,128)(2,1)} %bitcast.25), kind=kOutput, calls=%fused_computation.2 | convolution fusion | flops 3759931392 | bytes 9699328 | tf_op jit(solution)/shard_map/dot_general | solution.py:30
  144.8 0.0 copy-start.2
  144.8 0.0 copy-start
  144.8 0.0 reduce-scatter.2.cloned.1.call-update
  144.8 0.2 all-gather.4.cloned.1.call-start
  145.1 0.4 copy-done.2
  145.5 0.6 fusion.3
  146.1 0.6 iota_compare_fusion
  146.8 48.8 %reduce-scatter.2.cloned.1.call-done = bf16[256,896]{0,1:T(8,128)(2,1)} async-done(((bf16[2048,896]{0,1:T(8,128)(2,1)}), bf16[256,896]{0,1:T(8,128)(2,1)}) %reduce-scatter.2.cloned.1.call-update) | async-done | bytes 458768 | tf_op jit(solution)/shard_map/reduce_scatter | solution.py:31
  195.6 1.1 convert_element_type.27
  196.7 0.0 copy-done
  196.7 0.9 multiply_convert_fusion.1
  197.6 0.8 pad_maximum_fusion.1
  198.4 0.0 all-gather.4.cloned.1.call-update
  199.1 2.6 copy.17
  201.7 54.5 %all-gather.4.cloned.1.call-done = bf16[2048,896]{0,1:T(8,128)(2,1)} async-done(((bf16[256,896]{0,1:T(8,128)(2,1)}), bf16[2048,896]{0,1:T(8,128)(2,1)}) %all-gather.4.cloned.1.call-update) | async-done | bytes 3670032 | tf_op jit(solution)/shard_map/all_gather | solution.py:42
  256.2 7.8 %fusion = bf16[1024,896]{0,1:T(8,128)(2,1)S(1)} fusion(bf16[1024,896]{0,1:T(8,128)(2,1)} %copy.17, bf16[2048,896]{0,1:T(8,128)(2,1)} %all-gather.4.cloned.1.call-done, bf16[2048,1024]{0,1:T(8,128)(2,1)} %bitcast.26, f32[]{:T(128)S(6)} %div.7), kind=kOutput, calls=%fused_computation.1 | convolution fusion | flops 3761766400 | bytes 11534340 | tf_op jit(solution)/shard_map/dot_general | solution.py:43
  264.1 1.4 fusion.4
Async XLA Ops:
  7.2 116.1 %all-gather.6.cloned.1.call-start = ((), (), s32[]{:S(2)}) async-start(), calls=%async_computation.4 | async-start | bytes 4325376 | tf_op jit(solution)/shard_map/all_gather | solution.py:18
  7.2 11.7 %collective-permute-start = (bf16[256,256]{1,0:T(8,128)(2,1)}, bf16[256,256]{1,0:T(8,128)(2,1)S(1)}, u32[]{:S(2)}, u32[]{:S(2)}) collective-permute-start(bf16[256,256]{1,0:T(8,128)(2,1)} %param.5), channel_id=1, source_target_pairs={{0,0},{1,1},{2,2},{3,3},{4,32},{5,33},{6,34},{7,35},{8,64},{9,65},... | collective-permute-start | bytes 393224 | tf_op jit(solution)/shard_map/ppermute | solution.py:17
  18.9 0.7 copy-start.1
  28.8 108.0 %all-to-all-start = ((bf16[32,32,896]{2,0,1:T(8,128)(2,1)}), bf16[32,32,896]{2,0,1:T(8,128)(2,1)S(1)}, u32[]{:S(2)}, u32[]{:S(2)}) async-start(bf16[32,32,896]{2,0,1:T(8,128)(2,1)} %copy.15), calls=%async_computation | async-start | bytes 3670016 | tf_op jit(solution)/shard_map/all_to_all | solution.py:27
  47.9 147.7 %reduce-scatter.2.cloned.1.call-start = ((), (), s32[]{:S(2)}) async-start(), calls=%async_computation.2 | async-start | bytes 4128768 | tf_op jit(solution)/shard_map/reduce_scatter | solution.py:31
  144.8 0.7 copy-start.2
  144.8 51.9 %copy-start = (bf16[256,448]{0,1:T(8,128)(2,1)S(1)}, bf16[256,448]{0,1:T(8,128)(2,1)}, u32[]{:S(2)}) copy-start(bf16[256,448]{0,1:T(8,128)(2,1)} %param.9) | copy-start | bytes 688132
  144.8 111.4 %all-gather.4.cloned.1.call-start = ((), (), s32[]{:S(2)}) async-start(), calls=%async_computation.3 | async-start | bytes 4128768 | tf_op jit(solution)/shard_map/all_gather | solution.py:42
Sparse Core Ops, SparseCore 0:
  19.7 103.4 all-gather.5
  145.0 50.5 reduce-scatter.1
  198.6 57.6 all-gather.3

commit v2 on v1

v2 whole, which is shorter than its diff:
```python
import jax
import jax.numpy as jnp
from jax import lax
from jax.experimental import pallas as pl
from jax.experimental.pallas import tpu as pltpu
from jax.sharding import PartitionSpec as P

MESH = pl.DeviceIdType.MESH
BF16 = jnp.bfloat16
F32 = jnp.float32
NY, NX, NZ = 4, 2, 8
NSEC, NSHARD = 8, 32
ROWS = 256
DEPTH = 32
WIDTH = 448
KDIM = DEPTH * NSHARD
CHUNKS = (256, 256, 256, 128)
NC = len(CHUNKS)
OFFSETS = (0, -1, 1, -2, 2, -3, 3, 4)
STAGES = "FBXEGKH"


def kernel(lengths_ref, states_ref, gate_ref, up_ref, upstream_ref, hidden_ref, new_gate_ref, new_up_ref, *scratch):
    it = iter(scratch)
    s_buf, st_buf = next(it), next(it)
    ws, wr, p, ra, rb, qs, rx, dg = [[next(it) for _ in range(NC)] for _ in range(8)]
    (perm_s, perm_r, ring_s, ring_r, xh_s, xh_r, core_s, core_r, w_s, w_r,
     a_s, a_r, b_s, b_r, x_s, x_r, g_s, g_r) = list(it)

    sec, shard = lax.axis_index("section"), lax.axis_index("shard")
    xl, y = lax.div(sec, NY), lax.rem(sec, NY)
    z, quarter = lax.div(shard, 4), lax.rem(shard, 4)
    xh, core = lax.div(quarter, 2), lax.rem(quarter, 2)
    xo = 1 - xl
    yp, ym, yo = lax.rem(y + 1, NY), lax.rem(y + NY - 1, NY), lax.rem(y + 2, NY)
    zp, zm = lax.rem(z + 1, NZ), lax.rem(z + NZ - 1, NZ)

    def sid(x_, y_):
        return x_ * NY + y_

    def shid(z_, xh_, c_):
        return z_ * 4 + xh_ * 2 + c_

    up_dev, down_dev, xl_dev = (sid(xl, yp), shard), (sid(xl, ym), shard), (sid(xo, y), shard)
    zp_dev, zm_dev = (sec, shid(zp, xh, core)), (sec, shid(zm, xh, core))
    xh_dev, core_dev = (sec, shid(z, 1 - xh, core)), (sec, shid(z, xh, 1 - core))
    perm_dev = (z, sec * 4 + quarter)
    moves = z != sec

    barrier = pltpu.get_barrier_semaphore()

    @pl.loop(1, NSHARD)
    def _(d):
        pl.semaphore_signal(barrier, inc=1, device_id=(sec, lax.rem(shard + d, NSHARD)), device_id_type=MESH)

    for dev in (up_dev, down_dev, xl_dev):
        pl.semaphore_signal(barrier, inc=1, device_id=dev, device_id_type=MESH)

    @pl.when(moves)
    def _():
        pl.semaphore_signal(barrier, inc=1, device_id=perm_dev, device_id_type=MESH)

    pl.semaphore_wait(barrier, NSHARD - 1 + 3 + jnp.where(moves, 1, 0))

    sent = []

    def send(src, dst, ss, rs, dev):
        copy = pltpu.make_async_remote_copy(
            src_ref=src, dst_ref=dst, send_sem=ss, recv_sem=rs, device_id=dev, device_id_type=MESH
        )
        copy.start()
        sent.append((src, ss))

    def wait(ref, sem):
        pltpu.make_async_copy(ref, ref, sem).wait()

    def rows_of(section):
        return pl.ds(pl.multiple_of(section * ROWS, ROWS), ROWS)

    def cols_of(qq):
        return pl.ds(pl.multiple_of(qq * 256, 256), 256)

    own_block = s_buf.at[rows_of(z), cols_of(quarter)]
    perm_dst = s_buf.at[rows_of(sec), cols_of(quarter)]

    @pl.when(moves)
    def _():
        pltpu.make_async_remote_copy(
            src_ref=states_ref, dst_ref=perm_dst, send_sem=perm_s, recv_sem=perm_r,
            device_id=perm_dev, device_id_type=MESH,
        ).start()

    @pl.when(jnp.logical_not(moves))
    def _():
        pltpu.make_async_copy(states_ref, own_block, perm_r).start()

    lane = lax.broadcasted_iota(jnp.int32, (DEPTH, 128), 1)

    @pl.loop(0, NSHARD // 2)
    def _(m):
        both = pl.ds(pl.multiple_of(m * 2 * WIDTH, 128), 2 * WIDTH)
        g = gate_ref[:, both].astype(F32)
        u = up_ref[:, both].astype(F32)
        for odd in range(2):
            if odd:
                gv, uv = pltpu.roll(g, WIDTH, 1), pltpu.roll(u, WIDTH, 1)
                last_u = u[:, 2 * WIDTH - 128:]
            else:
                gv, uv = g, u
                last_u = pltpu.roll(u[:, 384:512], 64, 1)
            for k in range(NC - 1):
                ws[k][2 * m + odd, :, 0:128] = gv[:, k * 128:(k + 1) * 128].astype(BF16)
                ws[k][2 * m + odd, :, 128:256] = uv[:, k * 128:(k + 1) * 128].astype(BF16)
            ws[NC - 1][2 * m + odd] = jnp.where(lane < 64, gv[:, 384:512], last_u).astype(BF16)

    own_rows = pl.ds(pl.multiple_of(shard * DEPTH, DEPTH), DEPTH)

    def send_weights(k):
        @pl.loop(0, NSHARD - 1)
        def _(i):
            half = lax.div(i, 2) + 1
            d = jnp.where(lax.rem(i, 2) == 0, half, NSHARD - half)
            to = lax.rem(shard + d, NSHARD)
            pltpu.make_async_remote_copy(
                src_ref=ws[k].at[to], dst_ref=wr[k].at[own_rows], send_sem=w_s.at[k], recv_sem=w_r.at[k],
                device_id=(sec, to), device_id_type=MESH,
            ).start()

        pltpu.make_async_copy(ws[k].at[shard], wr[k].at[own_rows], w_r.at[k]).start()

    def block(off, qq):
        return s_buf.at[rows_of(lax.rem(z + off + NZ, NZ)), cols_of(qq)]

    def half_block(off, which):
        start = lax.rem(z + off + NZ, NZ) * ROWS + which * (ROWS // 2)
        return s_buf.at[pl.ds(pl.multiple_of(start, ROWS // 2), ROWS // 2), cols_of(quarter)]

    def share(i):
        ref = block(OFFSETS[i], quarter)
        send(ref, ref, xh_s.at[i], xh_r.at[i], xh_dev)
        send(ref, ref, core_s.at[0, i], core_r.at[0, i], core_dev)

    send_weights(0)
    wait(own_block, perm_r)
    send(own_block, own_block, ring_s.at[0, 0], ring_r.at[0, 0], zp_dev)
    send(own_block, own_block, ring_s.at[1, 0], ring_r.at[1, 0], zm_dev)
    share(0)
    for t in range(1, 4):
        for way in range(2):
            i = 2 * t - 1 + way
            ref = block(OFFSETS[i], quarter)
            wait(ref, ring_r.at[way, t - 1])
            onward = ref if t < 3 else half_block(OFFSETS[i], way)
            send(onward, onward, ring_s.at[way, t], ring_r.at[way, t], (zp_dev, zm_dev)[way])
            share(i)
        if t == 2:
            send_weights(1)
    for way in range(2):
        wait(half_block(4, way), ring_r.at[way, 3])
    share(7)
    send_weights(2)
    send_weights(3)
    partner = (1 - xh) * 2 + core
    for i in range(8):
        ref = block(OFFSETS[i], partner)
        wait(ref, xh_r.at[i])
        send(ref, ref, core_s.at[1, i], core_r.at[1, i], core_dev)
    for part in range(2):
        for i in range(8):
            qq = (xh if part == 0 else 1 - xh) * 2 + 1 - core
            wait(block(OFFSETS[i], qq), core_r.at[part, i])

    total = lengths_ref[0]
    for i in range(1, NSEC):
        total = total + lengths_ref[i]
    own_length = lengths_ref[sec]
    live = lax.broadcasted_iota(jnp.int32, (ROWS, 128), 0) < own_length

    def forward(k, section):
        r = rows_of(section)
        p[k][r, :] = jnp.dot(s_buf[r, :], wr[k][...], preferred_element_type=F32).astype(BF16)

    def stage_f(k):
        wait(wr[k], w_r.at[k])

        @pl.loop(0, 2)
        def _(i):
            forward(k, sid(i, yo))

        def part(x_, y_):
            return p[k].at[rows_of(sid(x_, y_))]

        send(part(0, yo), ra[k].at[0], a_s.at[k, 0], a_r.at[k, 0], up_dev)
        send(part(1, yo), ra[k].at[1], a_s.at[k, 1], a_r.at[k, 1], down_dev)

        @pl.loop(0, 4)
        def _(i):
            forward(k, sid(lax.rem(i, 2), jnp.where(i < 2, yp, ym)))

        send(part(1, yp), rb[k].at[1], b_s.at[k, 1], b_r.at[k, 1], up_dev)
        send(part(0, ym), rb[k].at[2], b_s.at[k, 2], b_r.at[k, 2], down_dev)

        @pl.loop(0, 2)
        def _(i):
            forward(k, sid(i, y))

    def stage_b(k):
        for way in range(2):
            wait(ra[k].at[way], a_r.at[k, way])
            r = rows_of(sid(way, (yp, ym)[way]))
            p[k][r, :] = (p[k][r, :].astype(F32) + ra[k][way].astype(F32)).astype(BF16)
            slot = (0, 3)[way]
            send(p[k].at[r], rb[k].at[slot], b_s.at[k, slot], b_r.at[k, slot], (up_dev, down_dev)[way])

    def stage_x(k):
        for slot in range(4):
            wait(rb[k].at[slot], b_r.at[k, slot])

        def summed(x_):
            r = rows_of(sid(x_, y))
            return p[k][r, :].astype(F32) + rb[k][x_].astype(F32) + rb[k][2 + x_].astype(F32)

        other = rows_of(sid(xo, y))
        p[k][other, :] = summed(xo).astype(BF16)
        send(p[k].at[other], rx[k], x_s.at[k], x_r.at[k], xl_dev)
        qs[k][...] = summed(xl)

    own_r = rows_of(sec)

    def grads(gate, upval, upstream, alive):
        sigma = 1.0 / (1.0 + jnp.exp(-gate))
        active = gate * sigma
        hid = (active * upval).astype(BF16)
        dh = jnp.where(alive, upstream.astype(F32), 0.0)
        d_gate = dh * upval * sigma * (1.0 + gate * (1.0 - sigma))
        return hid, d_gate, dh * active

    def stage_e(k):
        wait(rx[k], x_r.at[k])
        val = qs[k][...] + rx[k][...].astype(F32)
        if k < NC - 1:
            cols = slice(k * 128, (k + 1) * 128)
            hid, d_gate, d_up = grads(val[:, :128], val[:, 128:], upstream_ref[:, cols], live)
            hidden_ref[:, cols] = hid
            dg[k][own_r, 0:128] = d_gate.astype(BF16)
            dg[k][own_r, 128:256] = d_up.astype(BF16)
        else:
            cols = slice(k * 128, k * 128 + 64)
            hid, d_gate, d_up = grads(
                val[:, :64], pltpu.roll(val, 64, 1)[:, :64], upstream_ref[:, cols], live[:, :64]
            )
            hidden_ref[:, cols] = hid
            dg[k][own_r, :] = jnp.concatenate([d_gate, d_up], 1).astype(BF16)
        ref = dg[k].at[own_r]
        for slot, dev in ((0, xl_dev), (1, up_dev), (2, down_dev)):
            send(ref, ref, g_s.at[k, slot], g_r.at[k, slot], dev)

    def grad_block(k, x_, y_):
        return dg[k].at[rows_of(sid(x_, y_))]

    def stage_g(k):
        ref = grad_block(k, xo, y)
        wait(ref, g_r.at[k, 0])
        send(ref, ref, g_s.at[k, 3], g_r.at[k, 3], up_dev)
        send(ref, ref, g_s.at[k, 4], g_r.at[k, 4], down_dev)

    def stage_k(k):
        ref = grad_block(k, xl, ym)
        wait(ref, g_r.at[k, 1])
        send(ref, ref, g_s.at[k, 5], g_r.at[k, 5], up_dev)
        ref = grad_block(k, xo, yp)
        wait(ref, g_r.at[k, 4])
        send(ref, ref, g_s.at[k, 6], g_r.at[k, 6], down_dev)

    scale = 0.5 / jnp.full((ROWS, 128), total.astype(F32), F32)

    def stage_h(k):
        wait(grad_block(k, xl, yp), g_r.at[k, 2])
        wait(grad_block(k, xo, ym), g_r.at[k, 3])
        wait(grad_block(k, xl, yo), g_r.at[k, 5])
        wait(grad_block(k, xo, yo), g_r.at[k, 6])

        @pl.loop(0, KDIM // ROWS)
        def _(i):
            r = rows_of(i)
            acc = jnp.dot(st_buf[r, :], dg[k][...], preferred_element_type=F32)
            old = wr[k][r, :].astype(F32)
            first = old[:, :128] - scale * acc[:, :128]
            if k < NC - 1:
                cols = slice(k * 128, (k + 1) * 128)
                new_gate_ref[r, cols] = first.astype(BF16)
                new_up_ref[r, cols] = (old[:, 128:] - scale * acc[:, 128:]).astype(BF16)
            else:
                cols = slice(k * 128, k * 128 + 64)
                new_gate_ref[r, cols] = first[:, :64].astype(BF16)
                new_up_ref[r, cols] = pltpu.roll(first, 64, 1)[:, :64].astype(BF16)

    run = {"F": stage_f, "B": stage_b, "X": stage_x, "E": stage_e, "G": stage_g, "K": stage_k, "H": stage_h}
    order = sorted((2 * k + n, -n, name, k) for k in range(NC) for n, name in enumerate(STAGES))
    for _, _, name, k in order:
        run[name](k)
        if name == "F" and k == 0:
            @pl.loop(0, NSEC)
            def _(i):
                r = rows_of(i)
                st_buf[:, r] = s_buf[r, :].T

    @pl.when(moves)
    def _():
        wait(states_ref, perm_s)

    for k in range(NC):
        gone = ws[k].at[pl.ds(0, NSHARD - 1)]
        wait(gone, w_s.at[k])
    for src, ss in sent:
        wait(src, ss)


def shards(states, lengths, gate_weight, up_weight, upstream):
    vmem = pl.BlockSpec(memory_space=pltpu.VMEM)
    dma = pltpu.SemaphoreType.DMA
    buffers = [pltpu.VMEM((NSEC * ROWS, KDIM), BF16), pltpu.VMEM((KDIM, NSEC * ROWS), BF16)]
    for shape, kind in (
        ((NSHARD, DEPTH), BF16), ((KDIM,), BF16), ((NSEC * ROWS,), BF16), ((2, ROWS), BF16), ((4, ROWS), BF16),
        ((ROWS,), F32), ((ROWS,), BF16), ((NSEC * ROWS,), BF16),
    ):
        buffers += [pltpu.VMEM(shape + (n,), kind) for n in CHUNKS]
    sems = [dma, dma, dma((2, 4)), dma((2, 4)), dma((8,)), dma((8,)), dma((2, 8)), dma((2, 8)), dma((NC,)), dma((NC,)),
            dma((NC, 2)), dma((NC, 2)), dma((NC, 4)), dma((NC, 4)), dma((NC,)), dma((NC,)), dma((NC, 7)), dma((NC, 7))]
    return pl.pallas_call(
        kernel,
        out_shape=(
            jax.ShapeDtypeStruct((ROWS, WIDTH), BF16),
            jax.ShapeDtypeStruct((KDIM, WIDTH), BF16),
            jax.ShapeDtypeStruct((KDIM, WIDTH), BF16),
        ),
        in_specs=[pl.BlockSpec(memory_space=pltpu.SMEM)] + [vmem] * 4,
        out_specs=(vmem, vmem, vmem),
        scratch_shapes=buffers + sems,
        compiler_params=pltpu.CompilerParams(collective_id=0, has_side_effects=True, vmem_limit_bytes=56 << 20),
        cost_estimate=pl.CostEstimate(flops=7516192768, bytes_accessed=8 << 20, transcendentals=ROWS * WIDTH),
        name="projection_pair",
    )(lengths, states, gate_weight, up_weight, upstream)


def solution(mesh):
    in_specs = (
        P("section", "shard"),
        P(),
        P(("section", "shard"), None),
        P(("section", "shard"), None),
        P("section", "shard"),
    )
    out_specs = (P("section", "shard"), P("section", "shard"), P("section", "shard"))
    return jax.shard_map(shards, mesh=mesh, in_specs=in_specs, out_specs=out_specs, check_vma=False)
```

time: 277 us -> 161 us (0.58); the launches traced: 272 us -> 161 us
  waiting for transfers between devices: 188 us -> 0 us
  Pallas kernels: 0 us -> 153 us
  starting transfers between devices: 22.4 us -> 0 us
  local copies, waits for them, and re-layouts: 25.8 us -> 7.12 us
  matrix products: 15.8 us -> 0 us
  between operations: 14.5 us -> 0.64 us
  other arithmetic: 5.92 us -> 0 us
    pallas_call x0 -> x1, Pallas kernels: none -> 153 us  [shards(): pl.pallas_call(kernel, out_shape=(jax.ShapeDtypeStruct((ROWS, WIDTH), BF1...]
    all_gather x2 -> x0, waiting for transfers between devices: 130 us -> none  [the longest x1 75.4 us: shards(): blocks = lax.all_gather(moved, 'shard', axis=0, tiled=False)]
    reduce_scatter x1 -> x0, waiting for transfers between devices: 48.8 us -> none  [shards(): lax.psum_scatter(partial, 'section', scatter_dimension=0, tiled=True)]
    all_to_all x1 -> x0, starting transfers between devices: 19.1 us -> none  [shards(): lax.all_to_all(both, 'shard', split_axis=1, concat_axis=0, tiled=True)]
    reshape x4 -> x0, local copies, waits for them, and re-layouts: 15.9 us -> none  [the longest x1 7.89 us: shards(): rows = blocks.reshape(sections, quarter, span, cols).transpose(0, 2, 1, 3)]
    dot_general x2 -> x0, matrix products: 15.8 us -> none  [the longest x1 8 us: shards(): jnp.dot(rows, both, preferred_element_type=jnp.float32).astype(jnp.bfloat16)]
    ppermute x1 -> x0, waiting for transfers between devices: 8.7 us -> none  [shards(): moved = lax.ppermute(states, ('section', 'shard'), perm)]
    pallas_call x0 -> x3, local copies, waits for them, and re-layouts: none -> 5.33 us  [shards(): pl.pallas_call(kernel, out_shape=(jax.ShapeDtypeStruct((ROWS, WIDTH), BF1...]
  transfers between devices with their start and end apart: 5 -> 0, of which waited for: 4 -> 0; matrix products, arithmetic and copies ran while one was open for 10% -> 0% of each run, Pallas kernels for 0% -> 0%
where the time goes in v2:
time: 161 us
  Pallas kernels  153 us (95%)
  local copies, waits for them, and re-layouts  7.12 us (4%)
    pallas_call x1, Pallas kernels, shards(): pl.pallas_call(kernel, out_shape=(jax.ShapeDtypeStruct((ROWS, WIDTH), BF1...  153 us
    pallas_call x3, local copies, waits for them, and re-layouts, shards(): pl.pallas_call(kernel, out_shape=(jax.ShapeDtypeStruct((ROWS, WIDTH), BF1...  5.33 us

profile of v2, /device:TPU:36, one launch (start us, length us, event | category | flops | bytes accessed | tf_op | source)
XLA Modules:
  0.0 161.1 jit_solution(15364184748988457698)
XLA Ops:
  0.6 1.8 %copy.8.upstream_ref = bf16[256,448]{1,0:T(8,128)(2,1)} copy(bf16[256,448]{0,1:T(8,128)(2,1)} %param.9) | data formatting | bytes 458752 | tf_op args[4]
  2.4 153.3 %projection_pair.1 = (bf16[256,448]{1,0:T(8,128)(2,1)}, bf16[1024,448]{1,0:T(8,128)(2,1)}, bf16[1024,448]{1,0:T(8,128)(2,1)}) custom-call(s32[8]{0:T(128)} %lengths_ref.1, bf16[256,256]{1,0:T(8,128)(2,1)} %states_ref.1, bf16[32,14336]{1,0:T(8,128)(2,1)} %gate_ref.1, bf16[32,14336]{1,0:T(8,128)(2,1)} %up_ref.1, bf16[256,448]{1,0:T(8,128)(2,1)} %copy.8.upstream_ref), custom_call_target="tpu_custom_call" | custom-call | flops 7516192768 | bytes 8388608 | tf_op jit(solution)/shard_map/projection_pair/pallas_call | solution.py:330
  155.8 1.8 %copy.9 = bf16[256,448]{0,1:T(8,128)(2,1)} copy(bf16[256,448]{1,0:T(8,128)(2,1)} %get-tuple-element.3) | data formatting | bytes 458752 | tf_op jit(solution)/shard_map/projection_pair/pallas_call | solution.py:330
  157.5 0.0 copy-start
  157.5 2.3 %copy.10 = bf16[1024,448]{0,1:T(8,128)(2,1)} copy(bf16[1024,448]{1,0:T(8,128)(2,1)} %get-tuple-element.4) | data formatting | bytes 1835008 | tf_op jit(solution)/shard_map/projection_pair/pallas_call | solution.py:330
  159.8 0.0 copy-done
  159.8 1.3 copy.11
Async XLA Ops:
  157.5 2.3 %copy-start = (bf16[1024,448]{1,0:T(8,128)(2,1)S(1)}, bf16[1024,448]{1,0:T(8,128)(2,1)}, u32[]{:S(2)}) copy-start(bf16[1024,448]{1,0:T(8,128)(2,1)} %get-tuple-element.5) | copy-start | bytes 2752516

commit v3 on v2

v3 whole, which is shorter than its diff:
```python
import jax
import jax.numpy as jnp
from jax import lax
from jax.experimental import pallas as pl
from jax.experimental.pallas import tpu as pltpu
from jax.sharding import PartitionSpec as P

MESH = pl.DeviceIdType.MESH
BF16 = jnp.bfloat16
F32 = jnp.float32
NY, NX, NZ = 4, 2, 8
NSEC, NSHARD = 8, 32
ROWS = 256
DEPTH = 32
WIDTH = 448
KDIM = DEPTH * NSHARD
UNITS = 64
TILES = (1, 1, 1, 1, 1, 1, 1)
NC = len(TILES)
FIRST = tuple(sum(TILES[:k]) for k in range(NC))
AHEAD = 2
LAG = 2
OFFSETS = (0, -1, 1, -2, 2, -3, 3, 4)
STAGES = "FBXEGKH"


def kernel(lengths_ref, states_hbm, gate_hbm, up_hbm, upstream_hbm, hidden_hbm, new_gate_hbm, new_up_hbm, *scratch):
    it = iter(scratch)
    gate_ref, up_ref, upstream_ref, hidden_ref, new_gate_ref, new_up_ref, stage, s_buf = [next(it) for _ in range(8)]
    ws, wr, wt, p, ra, rb, qs, rx, dg = [[next(it) for _ in range(NC)] for _ in range(9)]
    (in_s, out_s, ring_s, ring_r, sec_s, sec_r, core_s, core_r, w_s, w_r,
     a_s, a_r, b_s, b_r, x_s, x_r, g_s, g_r) = list(it)

    sec, shard = lax.axis_index("section"), lax.axis_index("shard")
    xl, y = lax.div(sec, NY), lax.rem(sec, NY)
    z, quarter = lax.div(shard, 4), lax.rem(shard, 4)
    xh, core = lax.div(quarter, 2), lax.rem(quarter, 2)
    xo = 1 - xl
    yp, ym, yo = lax.rem(y + 1, NY), lax.rem(y + NY - 1, NY), lax.rem(y + 2, NY)
    zp, zm = lax.rem(z + 1, NZ), lax.rem(z + NZ - 1, NZ)

    def sid(x_, y_):
        return x_ * NY + y_

    def shid(z_, xh_, c_):
        return z_ * 4 + xh_ * 2 + c_

    up_dev, down_dev, xl_dev = (sid(xl, yp), shard), (sid(xl, ym), shard), (sid(xo, y), shard)
    zp_dev, zm_dev = (sec, shid(zp, xh, core)), (sec, shid(zm, xh, core))
    core_dev = (sec, shid(z, xh, 1 - core))

    barrier = pltpu.get_barrier_semaphore()

    @pl.loop(1, NSEC)
    def _(d):
        to = lax.rem(sec + d, NSEC)
        pl.semaphore_signal(barrier, inc=1, device_id=(to, shard), device_id_type=MESH)
        pl.semaphore_signal(barrier, inc=1, device_id=(to, shid(z, 1 - xh, core)), device_id_type=MESH)

    @pl.loop(1, NSHARD)
    def _(d):
        pl.semaphore_signal(barrier, inc=1, device_id=(sec, lax.rem(shard + d, NSHARD)), device_id_type=MESH)

    loads = [
        pltpu.make_async_copy(src, dst, in_s.at[i])
        for i, (src, dst) in enumerate((
            (states_hbm, stage.at[z]), (gate_hbm, gate_ref), (up_hbm, up_ref), (upstream_hbm, upstream_ref),
        ))
    ]
    for copy in loads:
        copy.start()

    sent = []

    def send(src, dst, ss, rs, dev):
        pltpu.make_async_remote_copy(
            src_ref=src, dst_ref=dst, send_sem=ss, recv_sem=rs, device_id=dev, device_id_type=MESH
        ).start()
        sent.append((src, ss))

    def wait(ref, sem):
        pltpu.make_async_copy(ref, ref, sem).wait()

    def rows_of(section):
        return pl.ds(pl.multiple_of(section * ROWS, ROWS), ROWS)

    def cols_of(qq):
        return pl.ds(pl.multiple_of(qq * 256, 256), 256)

    lane = lax.broadcasted_iota(jnp.int32, (DEPTH, 128), 1)
    loads[1].wait()
    loads[2].wait()

    @pl.loop(0, NSHARD // 2)
    def _(m):
        for k in range(NC):
            for t in range(TILES[k]):
                for odd in range(2):
                    a = odd * (WIDTH // UNITS) + FIRST[k] + t
                    cols = pl.ds(pl.multiple_of(m * 2 * WIDTH + (a // 2) * 128, 128), 128)
                    g, u = gate_ref[:, cols].astype(F32), up_ref[:, cols].astype(F32)
                    if a % 2:
                        val = jnp.where(lane < UNITS, pltpu.roll(g, UNITS, 1), u)
                    else:
                        val = jnp.where(lane < UNITS, g, pltpu.roll(u, UNITS, 1))
                    ws[k][2 * m + odd, :, t * 128:(t + 1) * 128] = val.astype(BF16)

    own_rows = pl.ds(pl.multiple_of(shard * DEPTH, DEPTH), DEPTH)

    def send_weights(k):
        @pl.loop(0, NSHARD - 1)
        def _(i):
            half = lax.div(i, 2) + 1
            d = jnp.where(lax.rem(i, 2) == 0, half, NSHARD - half)
            to = lax.rem(shard + d, NSHARD)
            pltpu.make_async_remote_copy(
                src_ref=ws[k].at[to], dst_ref=wr[k].at[own_rows], send_sem=w_s.at[k], recv_sem=w_r.at[k],
                device_id=(sec, to), device_id_type=MESH,
            ).start()

        pltpu.make_async_copy(ws[k].at[shard], wr[k].at[own_rows], w_r.at[k]).start()

    loads[0].wait()
    pl.semaphore_wait(barrier, NSHARD - 1 + 2 * (NSEC - 1))

    def zed(off):
        return lax.rem(z + off + NZ, NZ)

    def half_block(off, which):
        return stage.at[zed(off), pl.ds(which * (ROWS // 2), ROWS // 2)]

    own_slot = s_buf.at[rows_of(sec), cols_of(quarter)]

    def dispatch(i):
        k = zed(OFFSETS[i])
        src = stage.at[k]

        @pl.when(k != sec)
        def _():
            pltpu.make_async_remote_copy(
                src_ref=src, dst_ref=own_slot, send_sem=sec_s.at[i, 0], recv_sem=sec_r.at[sec, xh],
                device_id=(k, shard), device_id_type=MESH,
            ).start()

        @pl.when(k == sec)
        def _():
            pltpu.make_async_copy(src, own_slot, sec_r.at[sec, xh]).start()

        send(src, own_slot, sec_s.at[i, 1], sec_r.at[sec, xh], (k, shid(z, 1 - xh, core)))

    send(stage.at[z], stage.at[z], ring_s.at[0, 0], ring_r.at[0, 0], zp_dev)
    send(stage.at[z], stage.at[z], ring_s.at[1, 0], ring_r.at[1, 0], zm_dev)
    dispatch(0)
    send_weights(0)
    for t in range(1, 4):
        for way in range(2):
            i = 2 * t - 1 + way
            ref = stage.at[zed(OFFSETS[i])]
            wait(ref, ring_r.at[way, t - 1])
            onward = ref if t < 3 else half_block(OFFSETS[i], way)
            send(onward, onward, ring_s.at[way, t], ring_r.at[way, t], (zp_dev, zm_dev)[way])
            dispatch(i)
    for way in range(2):
        wait(half_block(4, way), ring_r.at[way, 3])
    dispatch(7)
    for k in range(1, AHEAD):
        send_weights(k)

    @pl.loop(0, NSEC)
    def _(d):
        s = lax.rem(sec + d, NSEC)
        for x_ in range(2):
            ref = s_buf.at[rows_of(s), cols_of(x_ * 2 + core)]
            wait(ref, sec_r.at[s, x_])
            pltpu.make_async_remote_copy(
                src_ref=ref, dst_ref=ref, send_sem=core_s.at[s, x_], recv_sem=core_r.at[s, x_],
                device_id=core_dev, device_id_type=MESH,
            ).start()

    @pl.loop(0, NSEC)
    def _(s):
        for x_ in range(2):
            wait(s_buf.at[rows_of(s), cols_of(x_ * 2 + 1 - core)], core_r.at[s, x_])

    loads[3].wait()
    total = lengths_ref[0]
    for i in range(1, NSEC):
        total = total + lengths_ref[i]
    live = lax.broadcasted_iota(jnp.int32, (UNITS, ROWS), 1) < lengths_ref[sec]
    scale = 0.5 / jnp.full((UNITS, 256), total.astype(F32), F32)

    def forward(k, section):
        acc = lax.dot_general(
            wt[k][...], s_buf[rows_of(section), :], (((1,), (1,)), ((), ())), preferred_element_type=F32
        )
        p[k][section] = acc.astype(BF16)

    def stage_f(k):
        wait(wr[k], w_r.at[k])
        if k + AHEAD < NC:
            send_weights(k + AHEAD)

        @pl.loop(0, KDIM // 256)
        def _(i):
            wt[k][:, cols_of(i)] = wr[k][cols_of(i), :].T

        @pl.loop(0, 2)
        def _(i):
            forward(k, sid(i, yo))

        send(p[k].at[sid(0, yo)], ra[k].at[0], a_s.at[k, 0], a_r.at[k, 0], up_dev)
        send(p[k].at[sid(1, yo)], ra[k].at[1], a_s.at[k, 1], a_r.at[k, 1], down_dev)

        @pl.loop(0, 4)
        def _(i):
            forward(k, sid(lax.rem(i, 2), jnp.where(i < 2, yp, ym)))

        send(p[k].at[sid(1, yp)], rb[k].at[1], b_s.at[k, 1], b_r.at[k, 1], up_dev)
        send(p[k].at[sid(0, ym)], rb[k].at[2], b_s.at[k, 2], b_r.at[k, 2], down_dev)

        @pl.loop(0, 2)
        def _(i):
            forward(k, sid(i, y))

    def stage_b(k):
        for way in range(2):
            wait(ra[k].at[way], a_r.at[k, way])
            s = sid(way, (yp, ym)[way])
            p[k][s] = (p[k][s].astype(F32) + ra[k][way].astype(F32)).astype(BF16)
            slot = (0, 3)[way]
            send(p[k].at[s], rb[k].at[slot], b_s.at[k, slot], b_r.at[k, slot], (up_dev, down_dev)[way])

    def stage_x(k):
        for slot in range(4):
            wait(rb[k].at[slot], b_r.at[k, slot])

        def summed(x_):
            return p[k][sid(x_, y)].astype(F32) + rb[k][x_].astype(F32) + rb[k][2 + x_].astype(F32)

        other = sid(xo, y)
        p[k][other] = summed(xo).astype(BF16)
        send(p[k].at[other], rx[k], x_s.at[k], x_r.at[k], xl_dev)
        qs[k][...] = summed(xl)

    def grad_block(k, x_, y_):
        return dg[k].at[:, rows_of(sid(x_, y_))]

    def stage_e(k):
        wait(rx[k], x_r.at[k])
        for t in range(TILES[k]):
            low, high = slice(t * 128, t * 128 + UNITS), slice(t * 128 + UNITS, (t + 1) * 128)
            units = slice((FIRST[k] + t) * UNITS, (FIRST[k] + t + 1) * UNITS)
            gate = qs[k][low] + rx[k][low].astype(F32)
            upval = qs[k][high] + rx[k][high].astype(F32)
            sigma = 1.0 / (1.0 + jnp.exp(-gate))
            active = gate * sigma
            hidden_ref[units] = (active * upval).astype(BF16)
            dh = jnp.where(live, upstream_ref[units].astype(F32), 0.0)
            d_gate = dh * upval * sigma * (1.0 + gate * (1.0 - sigma))
            dg[k][low, rows_of(sec)] = d_gate.astype(BF16)
            dg[k][high, rows_of(sec)] = (dh * active).astype(BF16)
        ref = grad_block(k, xl, y)
        for slot, dev in ((0, xl_dev), (1, up_dev), (2, down_dev)):
            send(ref, ref, g_s.at[k, slot], g_r.at[k, slot], dev)

    def stage_g(k):
        ref = grad_block(k, xo, y)
        wait(ref, g_r.at[k, 0])
        send(ref, ref, g_s.at[k, 3], g_r.at[k, 3], up_dev)
        send(ref, ref, g_s.at[k, 4], g_r.at[k, 4], down_dev)

    def stage_k(k):
        ref = grad_block(k, xl, ym)
        wait(ref, g_r.at[k, 1])
        send(ref, ref, g_s.at[k, 5], g_r.at[k, 5], up_dev)
        ref = grad_block(k, xo, yp)
        wait(ref, g_r.at[k, 4])
        send(ref, ref, g_s.at[k, 6], g_r.at[k, 6], down_dev)

    stores = []

    def stage_h(k):
        wait(grad_block(k, xl, yp), g_r.at[k, 2])
        wait(grad_block(k, xo, ym), g_r.at[k, 3])
        wait(grad_block(k, xl, yo), g_r.at[k, 5])
        wait(grad_block(k, xo, yo), g_r.at[k, 6])

        @pl.loop(0, KDIM // 256)
        def _(i):
            cols = cols_of(i)
            acc = jnp.dot(dg[k][...], s_buf[:, cols], preferred_element_type=F32)
            for t in range(TILES[k]):
                low, high = slice(t * 128, t * 128 + UNITS), slice(t * 128 + UNITS, (t + 1) * 128)
                units = slice((FIRST[k] + t) * UNITS, (FIRST[k] + t + 1) * UNITS)
                new_gate_ref[units, cols] = (wt[k][low, cols].astype(F32) - scale * acc[low]).astype(BF16)
                new_up_ref[units, cols] = (wt[k][high, cols].astype(F32) - scale * acc[high]).astype(BF16)

        part = pl.ds(FIRST[k] * UNITS, TILES[k] * UNITS)
        for n, (src, dst) in enumerate(((hidden_ref, hidden_hbm), (new_gate_ref, new_gate_hbm), (new_up_ref, new_up_hbm))):
            copy = pltpu.make_async_copy(src.at[part], dst.at[part], out_s.at[k, n])
            copy.start()
            stores.append(copy)

    run = {"F": stage_f, "B": stage_b, "X": stage_x, "E": stage_e, "G": stage_g, "K": stage_k, "H": stage_h}
    order = sorted((LAG * k + n, -n, name, k) for k in range(NC) for n, name in enumerate(STAGES))
    for _, _, name, k in order:
        run[name](k)

    for i in range(NZ):
        @pl.when(zed(OFFSETS[i]) != sec)
        def _():
            wait(stage.at[0], sec_s.at[i, 0])

    @pl.loop(0, NSEC)
    def _(s):
        for x_ in range(2):
            wait(stage.at[0], core_s.at[s, x_])

    for k in range(NC):
        wait(ws[k].at[pl.ds(0, NSHARD - 1)], w_s.at[k])
    for src, ss in sent:
        wait(src, ss)
    for copy in stores:
        copy.wait()


def shards(states, lengths, gate_weight, up_weight, upstream):
    hbm = pl.BlockSpec(memory_space=pl.ANY)
    dma = pltpu.SemaphoreType.DMA
    buffers = [
        pltpu.VMEM(shape, BF16)
        for shape in (
            (DEPTH, WIDTH * NSHARD), (DEPTH, WIDTH * NSHARD), (WIDTH, ROWS), (WIDTH, ROWS), (WIDTH, KDIM), (WIDTH, KDIM),
            (NZ, ROWS, 256), (NSEC * ROWS, KDIM),
        )
    ]
    sizes = [128 * t for t in TILES]
    for shape, kind in (
        (lambda n: (NSHARD, DEPTH, n), BF16), (lambda n: (KDIM, n), BF16), (lambda n: (n, KDIM), BF16),
        (lambda n: (NSEC, n, ROWS), BF16), (lambda n: (2, n, ROWS), BF16), (lambda n: (4, n, ROWS), BF16),
        (lambda n: (n, ROWS), F32), (lambda n: (n, ROWS), BF16), (lambda n: (n, NSEC * ROWS), BF16),
    ):
        buffers += [pltpu.VMEM(shape(n), kind) for n in sizes]
    sems = [dma((4,)), dma((NC, 3)), dma((2, 4)), dma((2, 4)), dma((NZ, 2)), dma((NSEC, 2)), dma((NSEC, 2)), dma((NSEC, 2)),
            dma((NC,)), dma((NC,)), dma((NC, 2)), dma((NC, 2)), dma((NC, 4)), dma((NC, 4)), dma((NC,)), dma((NC,)),
            dma((NC, 7)), dma((NC, 7))]
    hidden, new_gate, new_up = pl.pallas_call(
        kernel,
        out_shape=(
            jax.ShapeDtypeStruct((WIDTH, ROWS), BF16),
            jax.ShapeDtypeStruct((WIDTH, KDIM), BF16),
            jax.ShapeDtypeStruct((WIDTH, KDIM), BF16),
        ),
        in_specs=[pl.BlockSpec(memory_space=pltpu.SMEM)] + [hbm] * 4,
        out_specs=(hbm, hbm, hbm),
        scratch_shapes=buffers + sems,
        compiler_params=pltpu.CompilerParams(collective_id=0, has_side_effects=True, vmem_limit_bytes=56 << 20),
        cost_estimate=pl.CostEstimate(flops=7516192768, bytes_accessed=8 << 20, transcendentals=ROWS * WIDTH),
        name="projection_pair",
    )(lengths, states, gate_weight, up_weight, upstream.T)
    return hidden.T, new_gate.T, new_up.T


def solution(mesh):
    in_specs = (
        P("section", "shard"),
        P(),
        P(("section", "shard"), None),
        P(("section", "shard"), None),
        P("section", "shard"),
    )
    out_specs = (P("section", "shard"), P("section", "shard"), P("section", "shard"))
    return jax.shard_map(shards, mesh=mesh, in_specs=in_specs, out_specs=out_specs, check_vma=False)
```

time: 161 us -> 162 us (level)
  the two profiles are of different devices: /device:TPU:36 before, /device:TPU:66 now
where the time goes in v3:
time: 162 us
  Pallas kernels  157 us (97%)
  local copies, waits for them, and re-layouts  4.81 us (3%)
    pallas_call x1, Pallas kernels, shards(): pl.pallas_call(kernel, out_shape=(jax.ShapeDtypeStruct((WIDTH, ROWS), BF1...  157 us
    unnamed x5, local copies, waits for them, and re-layouts  4.81 us

profile of v3, /device:TPU:66, one launch (start us, length us, event | category | flops | bytes accessed | tf_op | source)
XLA Modules:
  0.0 162.2 jit_solution(3753494648358124374)
XLA Ops:
  0.6 156.7 %projection_pair.1 = (bf16[448,256]{1,0:T(8,128)(2,1)}, bf16[448,1024]{1,0:T(8,128)(2,1)}, bf16[448,1024]{1,0:T(8,128)(2,1)}) custom-call(s32[8]{0:T(128)} %lengths_ref.1, bf16[256,256]{1,0:T(8,128)(2,1)} %states_hbm.1, bf16[32,14336]{1,0:T(8,128)(2,1)} %gate_hbm.1, bf16[32,14336]{1,0:T(8,128)(2,1)} %up_hbm.1, bf16[448,256]{1,0:T(8,128)(2,1)} %bitcast.7), custom_call_target="tpu_custom_call" | custom-call | flops 7516192768 | bytes 8388608 | tf_op jit(solution)/shard_map/projection_pair/pallas_call | solution.py:347
  157.3 1.6 %copy.11 = bf16[256,448]{0,1:T(8,128)(2,1)} copy(bf16[256,448]{0,1:T(8,128)(2,1)} %bitcast.6) | data formatting | bytes 458752
  159.0 0.0 copy-start
  159.0 2.2 %copy.12 = bf16[1024,448]{0,1:T(8,128)(2,1)} copy(bf16[1024,448]{0,1:T(8,128)(2,1)} %bitcast.5) | data formatting | bytes 1835008
  161.2 0.0 copy-done
  161.2 0.9 copy.13
Async XLA Ops:
  159.0 2.2 %copy-start = (bf16[448,1024]{1,0:T(8,128)(2,1)S(1)}, bf16[448,1024]{1,0:T(8,128)(2,1)}, u32[]{:S(2)}) copy-start(bf16[448,1024]{1,0:T(8,128)(2,1)} %get-tuple-element.8) | copy-start | bytes 2752516

commit v4 on v3

v4 whole, which is shorter than its diff:
```python
import jax
import jax.numpy as jnp
from jax import lax
from jax.experimental import pallas as pl
from jax.experimental.pallas import tpu as pltpu
from jax.sharding import PartitionSpec as P

MESH = pl.DeviceIdType.MESH
BF16 = jnp.bfloat16
F32 = jnp.float32
NY, NX, NZ = 4, 2, 8
NSEC, NSHARD = 8, 32
ROWS = 256
DEPTH = 32
WIDTH = 448
KDIM = DEPTH * NSHARD
UNITS = 64
TILES = (1, 2, 2, 2)
NC = len(TILES)
FIRST = tuple(sum(TILES[:k]) for k in range(NC))
AHEAD = 2
LAG = 1
OFFSETS = (0, -1, 1, -2, 2, -3, 3, 4)
STAGES = "FBXEGKH"


def kernel(lengths_ref, states_ref, gate_ref, up_ref, upstream_ref, hidden_ref, new_gate_ref, new_up_ref, *scratch):
    it = iter(scratch)
    mid, s_buf, st_buf, acc = [next(it) for _ in range(4)]
    ws, wr, wt, p, ra, rb, qs, rx, dg = [[next(it) for _ in range(NC)] for _ in range(9)]
    (mid_s, mid_r, ring_s, ring_r, far_s, far_r, xh_s, xh_r, core_s, core_r, w_s, w_r,
     a_s, a_r, b_s, b_r, x_s, x_r, g_s, g_r) = list(it)

    sec, shard = lax.axis_index("section"), lax.axis_index("shard")
    xl, y = lax.div(sec, NY), lax.rem(sec, NY)
    z, quarter = lax.div(shard, 4), lax.rem(shard, 4)
    xh, core = lax.div(quarter, 2), lax.rem(quarter, 2)
    xo = 1 - xl
    yp, ym, yo = lax.rem(y + 1, NY), lax.rem(y + NY - 1, NY), lax.rem(y + 2, NY)
    zp, zm = lax.rem(z + 1, NZ), lax.rem(z + NZ - 1, NZ)

    def sid(x_, y_):
        return x_ * NY + y_

    def shid(z_, xh_, c_):
        return z_ * 4 + xh_ * 2 + c_

    up_dev, down_dev, xl_dev = (sid(xl, yp), shard), (sid(xl, ym), shard), (sid(xo, y), shard)
    zp_dev, zm_dev = (sec, shid(zp, xh, core)), (sec, shid(zm, xh, core))
    core_dev, xh_dev = (sec, shid(z, xh, 1 - core)), (sec, shid(z, 1 - xh, core))
    mid_dev, goal = (sec, shid(lax.rem(z + sec, NZ), xh, core)), lax.rem(z - sec + NZ, NZ)

    barrier = pltpu.get_barrier_semaphore()

    @pl.loop(1, NSEC)
    def _(d):
        to = lax.rem(sec + d, NSEC)
        pl.semaphore_signal(barrier, inc=1, device_id=(to, shard), device_id_type=MESH)

    @pl.loop(1, NSHARD)
    def _(d):
        pl.semaphore_signal(barrier, inc=1, device_id=(sec, lax.rem(shard + d, NSHARD)), device_id_type=MESH)

    sent = []

    def send(src, dst, ss, rs, dev):
        pltpu.make_async_remote_copy(
            src_ref=src, dst_ref=dst, send_sem=ss, recv_sem=rs, device_id=dev, device_id_type=MESH
        ).start()
        sent.append((src, ss))

    def wait(ref, sem):
        pltpu.make_async_copy(ref, ref, sem).wait()

    def slot_of(section):
        return lax.rem(section, NY) * NX + lax.div(section, NY)

    def rows_of(section):
        return pl.ds(pl.multiple_of(slot_of(section) * ROWS, ROWS), ROWS)

    def pair_of(y_):
        return pl.ds(pl.multiple_of(y_ * NX * ROWS, NX * ROWS), NX * ROWS)

    def cols_of(qq):
        return pl.ds(pl.multiple_of(qq * 256, 256), 256)

    lane = lax.broadcasted_iota(jnp.int32, (DEPTH, 128), 1)

    @pl.loop(0, NSHARD // 2)
    def _(m):
        for k in range(NC):
            for t in range(TILES[k]):
                for odd in range(2):
                    a = odd * (WIDTH // UNITS) + FIRST[k] + t
                    cols = pl.ds(pl.multiple_of(m * 2 * WIDTH + (a // 2) * 128, 128), 128)
                    g, u = gate_ref[:, cols].astype(F32), up_ref[:, cols].astype(F32)
                    if a % 2:
                        val = jnp.where(lane < UNITS, pltpu.roll(g, UNITS, 1), u)
                    else:
                        val = jnp.where(lane < UNITS, g, pltpu.roll(u, UNITS, 1))
                    ws[k][2 * m + odd, :, t * 128:(t + 1) * 128] = val.astype(BF16)

    own_rows = pl.ds(pl.multiple_of(shard * DEPTH, DEPTH), DEPTH)

    def send_weights(k):
        @pl.loop(0, NSHARD - 1)
        def _(i):
            half = lax.div(i, 2) + 1
            d = jnp.where(lax.rem(i, 2) == 0, half, NSHARD - half)
            to = lax.rem(shard + d, NSHARD)
            pltpu.make_async_remote_copy(
                src_ref=ws[k].at[to], dst_ref=wr[k].at[own_rows], send_sem=w_s.at[k], recv_sem=w_r.at[k],
                device_id=(sec, to), device_id_type=MESH,
            ).start()

        pltpu.make_async_copy(ws[k].at[shard], wr[k].at[own_rows], w_r.at[k]).start()

    pl.semaphore_wait(barrier, NSHARD - 1 + NSEC - 1)

    @pl.when(sec != 0)
    def _():
        pltpu.make_async_remote_copy(
            src_ref=states_ref, dst_ref=mid, send_sem=mid_s.at[0], recv_sem=mid_r.at[0],
            device_id=mid_dev, device_id_type=MESH,
        ).start()

    @pl.when(sec == 0)
    def _():
        pltpu.make_async_copy(states_ref, mid, mid_r.at[0]).start()

    def block(off, qq):
        return s_buf.at[rows_of(lax.rem(goal + off + NZ, NZ)), cols_of(qq)]

    def half_block(off, which, qq):
        start = slot_of(lax.rem(goal + off + NZ, NZ)) * ROWS + which * (ROWS // 2)
        return s_buf.at[pl.ds(pl.multiple_of(start, ROWS // 2), ROWS // 2), cols_of(qq)]

    partner = (1 - xh) * 2 + core
    z_devs = (zp_dev, zm_dev)

    def share(i, part):
        ref = block(OFFSETS[i], (quarter, partner)[part])
        if part == 0 and i < 5:
            send(ref, ref, xh_s.at[i], xh_r.at[i], xh_dev)
        send(ref, ref, core_s.at[part, i], core_r.at[part, i], core_dev)

    def onward(i, way, half, qq, ss, rs):
        ref = half_block(OFFSETS[i], way, qq) if half else block(OFFSETS[i], qq)
        send(ref, ref, ss, rs, z_devs[way])

    send_weights(0)
    wait(mid, mid_r.at[0])
    to_rows = s_buf.at[rows_of(sec), cols_of(quarter)]

    @pl.when(goal != sec)
    def _():
        pltpu.make_async_remote_copy(
            src_ref=mid, dst_ref=to_rows, send_sem=mid_s.at[1], recv_sem=mid_r.at[1],
            device_id=(goal, shard), device_id_type=MESH,
        ).start()

    @pl.when(goal == sec)
    def _():
        pltpu.make_async_copy(mid, to_rows, mid_r.at[1]).start()

    wait(block(0, quarter), mid_r.at[1])
    for way in range(2):
        onward(0, way, False, quarter, ring_s.at[way, 0], ring_r.at[way, 0])
    share(0, 0)
    for t in range(1, 4):
        for way in range(2):
            i = 2 * t - 1 + way
            wait(block(OFFSETS[i], quarter), ring_r.at[way, t - 1])
            onward(i, way, t == 3, quarter, ring_s.at[way, t], ring_r.at[way, t])
            share(i, 0)
    for i in range(5):
        wait(block(OFFSETS[i], partner), xh_r.at[i])
        if i > 2:
            onward(i, i - 3, False, partner, far_s.at[i - 3, 0], far_r.at[i - 3, 0])
        share(i, 1)
    for way in range(2):
        wait(half_block(4, way, quarter), ring_r.at[way, 3])
    share(7, 0)
    for way in range(2):
        wait(block(OFFSETS[5 + way], partner), far_r.at[way, 0])
        onward(5 + way, way, True, partner, far_s.at[way, 1], far_r.at[way, 1])
        share(5 + way, 1)
    for k in range(1, AHEAD):
        send_weights(k)
    for way in range(2):
        wait(half_block(4, way, partner), far_r.at[way, 1])
    share(7, 1)
    for part in range(2):
        for i in range(8):
            wait(block(OFFSETS[i], (quarter, partner)[part] + 1 - 2 * core), core_r.at[part, i])

    total = lengths_ref[0]
    for i in range(1, NSEC):
        total = total + lengths_ref[i]
    live = lax.broadcasted_iota(jnp.int32, (UNITS, ROWS), 1) < lengths_ref[sec]
    scale = 0.5 / jnp.full((UNITS, 256), total.astype(F32), F32)

    def forward(k, y_):
        p[k][pair_of(y_), :] = jnp.dot(s_buf[pair_of(y_), :], wr[k][...], preferred_element_type=F32).astype(BF16)

    def part(k, x_, y_):
        return p[k].at[rows_of(sid(x_, y_))]

    def stage_f(k):
        wait(wr[k], w_r.at[k])
        if k + AHEAD < NC:
            send_weights(k + AHEAD)

        forward(k, yo)
        send(part(k, 0, yo), ra[k].at[0], a_s.at[k, 0], a_r.at[k, 0], up_dev)
        send(part(k, 1, yo), ra[k].at[1], a_s.at[k, 1], a_r.at[k, 1], down_dev)
        forward(k, yp)
        send(part(k, 1, yp), rb[k].at[1], b_s.at[k, 1], b_r.at[k, 1], up_dev)
        forward(k, ym)
        send(part(k, 0, ym), rb[k].at[2], b_s.at[k, 2], b_r.at[k, 2], down_dev)
        forward(k, y)

        @pl.loop(0, KDIM // 256)
        def _(i):
            wt[k][:, cols_of(i)] = wr[k][cols_of(i), :].T

    def stage_b(k):
        for way in range(2):
            wait(ra[k].at[way], a_r.at[k, way])
            r = rows_of(sid(way, (yp, ym)[way]))
            p[k][r, :] = (p[k][r, :].astype(F32) + ra[k][way].astype(F32)).astype(BF16)
            slot = (0, 3)[way]
            send(p[k].at[r], rb[k].at[slot], b_s.at[k, slot], b_r.at[k, slot], (up_dev, down_dev)[way])

    def stage_x(k):
        for slot in range(4):
            wait(rb[k].at[slot], b_r.at[k, slot])

        def summed(x_):
            r = rows_of(sid(x_, y))
            return p[k][r, :].astype(F32) + rb[k][x_].astype(F32) + rb[k][2 + x_].astype(F32)

        other = rows_of(sid(xo, y))
        p[k][other, :] = summed(xo).astype(BF16)
        send(p[k].at[other], rx[k], x_s.at[k], x_r.at[k], xl_dev)
        qs[k][...] = summed(xl)

    def grad_block(k, x_, y_):
        return dg[k].at[rows_of(sid(x_, y_))]

    def stage_e(k):
        wait(rx[k], x_r.at[k])
        val = (qs[k][...] + rx[k][...].astype(F32)).T
        pieces = []
        for t in range(TILES[k]):
            units = slice((FIRST[k] + t) * UNITS, (FIRST[k] + t + 1) * UNITS)
            gate, upval = val[t * 128:t * 128 + UNITS], val[t * 128 + UNITS:(t + 1) * 128]
            sigma = 1.0 / (1.0 + jnp.exp(-gate))
            active = gate * sigma
            hidden_ref[units] = (active * upval).astype(BF16)
            dh = jnp.where(live, upstream_ref[units].astype(F32), 0.0)
            pieces += [dh * upval * sigma * (1.0 + gate * (1.0 - sigma)), dh * active]
        dg[k][rows_of(sec), :] = jnp.concatenate(pieces, 0).T.astype(BF16)
        ref = grad_block(k, xl, y)
        for slot, dev in ((0, xl_dev), (1, up_dev), (2, down_dev)):
            send(ref, ref, g_s.at[k, slot], g_r.at[k, slot], dev)

    def stage_g(k):
        ref = grad_block(k, xo, y)
        wait(ref, g_r.at[k, 0])
        send(ref, ref, g_s.at[k, 3], g_r.at[k, 3], up_dev)
        send(ref, ref, g_s.at[k, 4], g_r.at[k, 4], down_dev)

    def stage_k(k):
        ref = grad_block(k, xl, ym)
        wait(ref, g_r.at[k, 1])
        send(ref, ref, g_s.at[k, 5], g_r.at[k, 5], up_dev)
        ref = grad_block(k, xo, yp)
        wait(ref, g_r.at[k, 4])
        send(ref, ref, g_s.at[k, 6], g_r.at[k, 6], down_dev)

    def stage_h(k):
        wait(grad_block(k, xl, yp), g_r.at[k, 2])
        wait(grad_block(k, xo, ym), g_r.at[k, 3])
        wait(grad_block(k, xl, yo), g_r.at[k, 5])
        wait(grad_block(k, xo, yo), g_r.at[k, 6])

        acc[:, 0:128 * TILES[k]] = jnp.dot(st_buf[...], dg[k][...], preferred_element_type=F32)

        @pl.loop(0, KDIM // 256)
        def _(i):
            cols = cols_of(i)
            turned = acc[cols, 0:128 * TILES[k]].T
            for t in range(TILES[k]):
                low, high = slice(t * 128, t * 128 + UNITS), slice(t * 128 + UNITS, (t + 1) * 128)
                units = slice((FIRST[k] + t) * UNITS, (FIRST[k] + t + 1) * UNITS)
                new_gate_ref[units, cols] = (wt[k][low, cols].astype(F32) - scale * turned[low]).astype(BF16)
                new_up_ref[units, cols] = (wt[k][high, cols].astype(F32) - scale * turned[high]).astype(BF16)

    run = {"F": stage_f, "B": stage_b, "X": stage_x, "E": stage_e, "G": stage_g, "K": stage_k, "H": stage_h}
    order = sorted((LAG * k + n, -n, name, k) for k in range(NC) for n, name in enumerate(STAGES))
    for _, _, name, k in order:
        run[name](k)
        if name == "F" and k == 0:
            @pl.loop(0, NSEC)
            def _(i):
                r = cols_of(i)
                st_buf[:, r] = s_buf[r, :].T

    @pl.when(sec != 0)
    def _():
        wait(mid, mid_s.at[0])

    @pl.when(goal != sec)
    def _():
        wait(mid, mid_s.at[1])

    for k in range(NC):
        wait(ws[k].at[pl.ds(0, NSHARD - 1)], w_s.at[k])
    for src, ss in sent:
        wait(src, ss)


def shards(states, lengths, gate_weight, up_weight, upstream):
    vmem = pl.BlockSpec(memory_space=pltpu.VMEM)
    dma = pltpu.SemaphoreType.DMA
    buffers = [
        pltpu.VMEM((ROWS, 256), BF16), pltpu.VMEM((NSEC * ROWS, KDIM), BF16), pltpu.VMEM((KDIM, NSEC * ROWS), BF16),
        pltpu.VMEM((KDIM, 128 * max(TILES)), F32),
    ]
    sizes = [128 * t for t in TILES]
    for shape, kind in (
        (lambda n: (NSHARD, DEPTH, n), BF16), (lambda n: (KDIM, n), BF16), (lambda n: (n, KDIM), BF16),
        (lambda n: (NSEC * ROWS, n), BF16), (lambda n: (2, ROWS, n), BF16), (lambda n: (4, ROWS, n), BF16),
        (lambda n: (ROWS, n), F32), (lambda n: (ROWS, n), BF16), (lambda n: (NSEC * ROWS, n), BF16),
    ):
        buffers += [pltpu.VMEM(shape(n), kind) for n in sizes]
    sems = [dma((2,)), dma((2,)), dma((2, 4)), dma((2, 4)), dma((2, 2)), dma((2, 2)), dma((5,)), dma((5,)), dma((2, 8)), dma((2, 8)),
            dma((NC,)), dma((NC,)), dma((NC, 2)), dma((NC, 2)), dma((NC, 4)), dma((NC, 4)), dma((NC,)), dma((NC,)),
            dma((NC, 7)), dma((NC, 7))]
    hidden, new_gate, new_up = pl.pallas_call(
        kernel,
        out_shape=(
            jax.ShapeDtypeStruct((WIDTH, ROWS), BF16),
            jax.ShapeDtypeStruct((WIDTH, KDIM), BF16),
            jax.ShapeDtypeStruct((WIDTH, KDIM), BF16),
        ),
        in_specs=[pl.BlockSpec(memory_space=pltpu.SMEM)] + [vmem] * 4,
        out_specs=(vmem, vmem, vmem),
        scratch_shapes=buffers + sems,
        compiler_params=pltpu.CompilerParams(collective_id=0, has_side_effects=True, vmem_limit_bytes=44 << 20),
        cost_estimate=pl.CostEstimate(flops=7516192768, bytes_accessed=8 << 20, transcendentals=ROWS * WIDTH),
        name="projection_pair",
    )(lengths, states, gate_weight, up_weight, upstream.T)
    return hidden.T, new_gate.T, new_up.T


def solution(mesh):
    in_specs = (
        P("section", "shard"),
        P(),
        P(("section", "shard"), None),
        P(("section", "shard"), None),
        P("section", "shard"),
    )
    out_specs = (P("section", "shard"), P("section", "shard"), P("section", "shard"))
    return jax.shard_map(shards, mesh=mesh, in_specs=in_specs, out_specs=out_specs, check_vma=False)
```

time: 162 us -> 144 us (0.89)
  the two profiles are of different devices: /device:TPU:66 before, /device:TPU:36 now
where the time goes in v4:
time: 144 us; the launch traced here: 143 us
  Pallas kernels  135 us (94%)
  local copies, waits for them, and re-layouts  7.38 us (5%)
    pallas_call x1, Pallas kernels, shards(): pl.pallas_call(kernel, out_shape=(jax.ShapeDtypeStruct((WIDTH, ROWS), BF1...  135 us
    unnamed x13, local copies, waits for them, and re-layouts  7.38 us

profile of v4, /device:TPU:36, one launch (start us, length us, event | category | flops | bytes accessed | tf_op | source)
XLA Modules:
  0.0 143.1 jit_solution(17784466915714858774)
XLA Ops:
  0.6 0.0 copy-start.4
  0.6 0.6 copy-done.4
  1.3 0.0 copy-start
  1.3 1.2 copy-done
  2.5 0.0 copy-start.1
  2.5 1.2 copy-done.1
  3.6 0.0 copy-start.2
  3.6 0.9 copy-done.2
  4.6 0.0 copy-start.3
  4.6 0.9 copy-done.3
  5.5 135.1 %projection_pair.1 = (bf16[448,256]{1,0:T(8,128)(2,1)S(1)}, bf16[448,1024]{1,0:T(8,128)(2,1)S(1)}, bf16[448,1024]{1,0:T(8,128)(2,1)S(1)}) custom-call(s32[8]{0:T(128)S(1)} %copy-done.4, bf16[256,256]{1,0:T(8,128)(2,1)S(1)} %copy-done.3, bf16[32,14336]{1,0:T(8,128)(2,1)S(1)} %copy-done, bf16[32,14336]{1,0:T(8,128)(2,1)S(1)} %copy-done.1, ...), custom_call_target="tpu_custom_call" | custom-call | flops 7516192768 | bytes 8388608 | tf_op jit(solution)/shard_map/projection_pair/pallas_call | solution.py:341
  140.6 0.7 copy.11
  141.3 0.9 copy.12
  142.2 0.9 copy.13
Async XLA Ops:
  0.6 0.7 copy-start.4
  1.3 1.2 copy-start
  2.5 1.2 copy-start.1
  3.6 0.9 copy-start.2
  4.6 0.9 copy-start.3

commit v5 on v4

--- a/solution.py
+++ b/solution.py
@@ -11,6 +11,7 @@
 NY, NX, NZ = 4, 2, 8
 NSEC, NSHARD = 8, 32
 ROWS = 256
+HALF = ROWS // 2
 DEPTH = 32
 WIDTH = 448
 KDIM = DEPTH * NSHARD
@@ -20,15 +21,16 @@
 FIRST = tuple(sum(TILES[:k]) for k in range(NC))
 AHEAD = 2
 LAG = 1
+EARLY = 4
 OFFSETS = (0, -1, 1, -2, 2, -3, 3, 4)
 STAGES = "FBXEGKH"
 
 
-def kernel(lengths_ref, states_ref, gate_ref, up_ref, upstream_ref, hidden_ref, new_gate_ref, new_up_ref, *scratch):
+def kernel(lengths_ref, states_hbm, gate_hbm, up_hbm, upstream_hbm, hidden_ref, new_gate_ref, new_up_ref, *scratch):
     it = iter(scratch)
-    mid, s_buf, st_buf, acc = [next(it) for _ in range(4)]
+    states_ref, gate_ref, up_ref, upstream_ref, mid, s_buf, st_buf, acc = [next(it) for _ in range(8)]
     ws, wr, wt, p, ra, rb, qs, rx, dg = [[next(it) for _ in range(NC)] for _ in range(9)]
-    (mid_s, mid_r, ring_s, ring_r, far_s, far_r, xh_s, xh_r, core_s, core_r, w_s, w_r,
+    (in_s, mid_s, mid_r, ring_s, ring_r, far_s, far_r, xh_s, xh_r, core_s, core_r, w_s, w_r,
      a_s, a_r, b_s, b_r, x_s, x_r, g_s, g_r) = list(it)
 
     sec, shard = lax.axis_index("section"), lax.axis_index("shard")
@@ -48,7 +50,16 @@
     up_dev, down_dev, xl_dev = (sid(xl, yp), shard), (sid(xl, ym), shard), (sid(xo, y), shard)
     zp_dev, zm_dev = (sec, shid(zp, xh, core)), (sec, shid(zm, xh, core))
     core_dev, xh_dev = (sec, shid(z, xh, 1 - core)), (sec, shid(z, 1 - xh, core))
-    mid_dev, goal = (sec, shid(lax.rem(z + sec, NZ), xh, core)), lax.rem(z - sec + NZ, NZ)
+
+    def crossed(z_):
+        out = 0
+        for bit in (1, 2, 4):
+            one, two = lax.rem(lax.div(z_, bit), 2), lax.rem(lax.div(sec, bit), 2)
+            out = out + bit * (one + two - 2 * one * two)
+        return out
+
+    goal = crossed(z)
+    mid_dev = (sec, shid(goal, xh, core))
 
     barrier = pltpu.get_barrier_semaphore()
 
@@ -60,6 +71,15 @@
     @pl.loop(1, NSHARD)
     def _(d):
         pl.semaphore_signal(barrier, inc=1, device_id=(sec, lax.rem(shard + d, NSHARD)), device_id_type=MESH)
+
+    loads = [
+        pltpu.make_async_copy(src, dst, in_s.at[i])
+        for i, (src, dst) in enumerate((
+            (states_hbm, states_ref), (gate_hbm, gate_ref), (up_hbm, up_ref), (upstream_hbm, upstream_ref),
+        ))
+    ]
+    for copy in loads:
+        copy.start()
 
     sent = []
 
@@ -84,7 +104,41 @@
     def cols_of(qq):
         return pl.ds(pl.multiple_of(qq * 256, 256), 256)
 
+    own_rows = pl.ds(pl.multiple_of(shard * DEPTH, DEPTH), DEPTH)
+
+    def send_weights(k):
+        @pl.loop(0, NSHARD - 1)
+        def _(i):
+            half = lax.div(i, 2) + 1
+            d = jnp.where(lax.rem(i, 2) == 0, half, NSHARD - half)
+            to = lax.rem(shard + d, NSHARD)
+            pltpu.make_async_remote_copy(
+                src_ref=ws[k].at[to], dst_ref=wr[k].at[own_rows], send_sem=w_s.at[k], recv_sem=w_r.at[k],
+                device_id=(sec, to), device_id_type=MESH,
+            ).start()
+
+        pltpu.make_async_copy(ws[k].at[shard], wr[k].at[own_rows], w_r.at[k]).start()
+
+    loads[0].wait()
+    pl.semaphore_wait(barrier, NSHARD - 1 + NSEC - 1)
+
+    for h in range(2):
+        part = pl.ds(h * HALF, HALF)
+
+        @pl.when(sec != 0)
+        def _():
+            pltpu.make_async_remote_copy(
+                src_ref=states_ref.at[part], dst_ref=mid.at[part], send_sem=mid_s.at[0, h], recv_sem=mid_r.at[0, h],
+                device_id=mid_dev, device_id_type=MESH,
+            ).start()
+
+        @pl.when(sec == 0)
+        def _():
+            pltpu.make_async_copy(states_ref.at[part], mid.at[part], mid_r.at[0, h]).start()
+
     lane = lax.broadcasted_iota(jnp.int32, (DEPTH, 128), 1)
+    loads[1].wait()
+    loads[2].wait()
 
     @pl.loop(0, NSHARD // 2)
     def _(m):
@@ -100,100 +154,89 @@
                         val = jnp.where(lane < UNITS, g, pltpu.roll(u, UNITS, 1))
                     ws[k][2 * m + odd, :, t * 128:(t + 1) * 128] = val.astype(BF16)
 
-    own_rows = pl.ds(pl.multiple_of(shard * DEPTH, DEPTH), DEPTH)
-
-    def send_weights(k):
-        @pl.loop(0, NSHARD - 1)
-        def _(i):
-            half = lax.div(i, 2) + 1
-            d = jnp.where(lax.rem(i, 2) == 0, half, NSHARD - half)
-            to = lax.rem(shard + d, NSHARD)
-            pltpu.make_async_remote_copy(
-                src_ref=ws[k].at[to], dst_ref=wr[k].at[own_rows], send_sem=w_s.at[k], recv_sem=w_r.at[k],
-                device_id=(sec, to), device_id_type=MESH,
-            ).start()
-
-        pltpu.make_async_copy(ws[k].at[shard], wr[k].at[own_rows], w_r.at[k]).start()
-
-    pl.semaphore_wait(barrier, NSHARD - 1 + NSEC - 1)
-
-    @pl.when(sec != 0)
-    def _():
-        pltpu.make_async_remote_copy(
-            src_ref=states_ref, dst_ref=mid, send_sem=mid_s.at[0], recv_sem=mid_r.at[0],
-            device_id=mid_dev, device_id_type=MESH,
-        ).start()
-
-    @pl.when(sec == 0)
-    def _():
-        pltpu.make_async_copy(states_ref, mid, mid_r.at[0]).start()
-
-    def block(off, qq):
-        return s_buf.at[rows_of(lax.rem(goal + off + NZ, NZ)), cols_of(qq)]
-
-    def half_block(off, which, qq):
-        start = slot_of(lax.rem(goal + off + NZ, NZ)) * ROWS + which * (ROWS // 2)
-        return s_buf.at[pl.ds(pl.multiple_of(start, ROWS // 2), ROWS // 2), cols_of(qq)]
+    def half_of(section, h, qq):
+        start = slot_of(section) * ROWS + h * HALF
+        return s_buf.at[pl.ds(pl.multiple_of(start, HALF), HALF), cols_of(qq)]
+
+    def piece(i, h, qq):
+        return half_of(crossed(lax.rem(z + OFFSETS[i] + NZ, NZ)), h, qq)
 
     partner = (1 - xh) * 2 + core
     z_devs = (zp_dev, zm_dev)
 
-    def share(i, part):
-        ref = block(OFFSETS[i], (quarter, partner)[part])
+    def share(i, h, part):
+        ref = piece(i, h, (quarter, partner)[part])
         if part == 0 and i < 5:
-            send(ref, ref, xh_s.at[i], xh_r.at[i], xh_dev)
-        send(ref, ref, core_s.at[part, i], core_r.at[part, i], core_dev)
-
-    def onward(i, way, half, qq, ss, rs):
-        ref = half_block(OFFSETS[i], way, qq) if half else block(OFFSETS[i], qq)
+            send(ref, ref, xh_s.at[i, h], xh_r.at[i, h], xh_dev)
+        send(ref, ref, core_s.at[part, i, h], core_r.at[part, i, h], core_dev)
+
+    def onward(i, h, way, qq, ss, rs):
+        ref = piece(i, h, qq)
         send(ref, ref, ss, rs, z_devs[way])
 
+    def near(i):
+        for h in range(2):
+            wait(piece(i, h, partner), xh_r.at[i, h])
+            if i > 2:
+                onward(i, h, i - 3, partner, far_s.at[i - 3, 0, h], far_r.at[i - 3, 0, h])
+            share(i, h, 1)
+
     send_weights(0)
-    wait(mid, mid_r.at[0])
-    to_rows = s_buf.at[rows_of(sec), cols_of(quarter)]
-
-    @pl.when(goal != sec)
-    def _():
-        pltpu.make_async_remote_copy(
-            src_ref=mid, dst_ref=to_rows, send_sem=mid_s.at[1], recv_sem=mid_r.at[1],
-            device_id=(goal, shard), device_id_type=MESH,
-        ).start()
-
-    @pl.when(goal == sec)
-    def _():
-        pltpu.make_async_copy(mid, to_rows, mid_r.at[1]).start()
-
-    wait(block(0, quarter), mid_r.at[1])
+    for h in range(2):
+        part = pl.ds(h * HALF, HALF)
+        wait(mid.at[part], mid_r.at[0, h])
+        to_rows = half_of(sec, h, quarter)
+
+        @pl.when(goal != sec)
+        def _():
+            pltpu.make_async_remote_copy(
+                src_ref=mid.at[part], dst_ref=to_rows, send_sem=mid_s.at[1, h], recv_sem=mid_r.at[1, h],
+                device_id=(goal, shard), device_id_type=MESH,
+            ).start()
+
+        @pl.when(goal == sec)
+        def _():
+            pltpu.make_async_copy(mid.at[part], to_rows, mid_r.at[1, h]).start()
+
+    for h in range(2):
+        wait(piece(0, h, quarter), mid_r.at[1, h])
+        for way in range(2):
+            onward(0, h, way, quarter, ring_s.at[way, 0, h], ring_r.at[way, 0, h])
+        share(0, h, 0)
+    for t in range(1, 4):
+        for h in range(2):
+            for way in range(2):
+                i = 2 * t - 1 + way
+                wait(piece(i, h, quarter), ring_r.at[way, t - 1, h])
+                if t < 3 or h == way:
+                    onward(i, h, way, quarter, ring_s.at[way, t, h], ring_r.at[way, t, h])
+                share(i, h, 0)
+        if t == EARLY:
+            for k in range(1, AHEAD):
+                send_weights(k)
+        for i in ((0,), (1, 2), (3, 4))[t - 1]:
+            near(i)
     for way in range(2):
-        onward(0, way, False, quarter, ring_s.at[way, 0], ring_r.at[way, 0])
-    share(0, 0)
-    for t in range(1, 4):
+        wait(piece(7, way, quarter), ring_r.at[way, 3, way])
+        share(7, way, 0)
+    for h in range(2):
         for way in range(2):
-            i = 2 * t - 1 + way
-            wait(block(OFFSETS[i], quarter), ring_r.at[way, t - 1])
-            onward(i, way, t == 3, quarter, ring_s.at[way, t], ring_r.at[way, t])
-            share(i, 0)
-    for i in range(5):
-        wait(block(OFFSETS[i], partner), xh_r.at[i])
-        if i > 2:
-            onward(i, i - 3, False, partner, far_s.at[i - 3, 0], far_r.at[i - 3, 0])
-        share(i, 1)
+            wait(piece(5 + way, h, partner), far_r.at[way, 0, h])
+            if h == way:
+                onward(5 + way, h, way, partner, far_s.at[way, 1, h], far_r.at[way, 1, h])
+            share(5 + way, h, 1)
+    if EARLY == 4:
+        for k in range(1, AHEAD):
+            send_weights(k)
     for way in range(2):
-        wait(half_block(4, way, quarter), ring_r.at[way, 3])
-    share(7, 0)
-    for way in range(2):
-        wait(block(OFFSETS[5 + way], partner), far_r.at[way, 0])
-        onward(5 + way, way, True, partner, far_s.at[way, 1], far_r.at[way, 1])
-        share(5 + way, 1)
-    for k in range(1, AHEAD):
-        send_weights(k)
-    for way in range(2):
-        wait(half_block(4, way, partner), far_r.at[way, 1])
-    share(7, 1)
+        wait(piece(7, way, partner), far_r.at[way, 1, way])
+        share(7, way, 1)
     for part in range(2):
         for i in range(8):
-            wait(block(OFFSETS[i], (quarter, partner)[part] + 1 - 2 * core), core_r.at[part, i])
-
+            for h in range(2):
+                wait(piece(i, h, (quarter, partner)[part] + 1 - 2 * core), core_r.at[part, i, h])
+
+    loads[3].wait()
     total = lengths_ref[0]
     for i in range(1, NSEC):
         total = total + lengths_ref[i]
@@ -309,11 +352,13 @@
 
     @pl.when(sec != 0)
     def _():
-        wait(mid, mid_s.at[0])
+        for h in range(2):
+            wait(mid.at[pl.ds(h * HALF, HALF)], mid_s.at[0, h])
 
     @pl.when(goal != sec)
     def _():
-        wait(mid, mid_s.at[1])
+        for h in range(2):
+            wait(mid.at[pl.ds(h * HALF, HALF)], mid_s.at[1, h])
 
     for k in range(NC):
         wait(ws[k].at[pl.ds(0, NSHARD - 1)], w_s.at[k])
@@ -325,7 +370,8 @@
     vmem = pl.BlockSpec(memory_space=pltpu.VMEM)
     dma = pltpu.SemaphoreType.DMA
     buffers = [
-        pltpu.VMEM((ROWS, 256), BF16), pltpu.VMEM((NSEC * ROWS, KDIM), BF16), pltpu.VMEM((KDIM, NSEC * ROWS), BF16),
+        pltpu.VMEM((ROWS, 256), BF16), pltpu.VMEM((DEPTH, WIDTH * NSHARD), BF16), pltpu.VMEM((DEPTH, WIDTH * NSHARD), BF16),
+        pltpu.VMEM((WIDTH, ROWS), BF16), pltpu.VMEM((ROWS, 256), BF16), pltpu.VMEM((NSEC * ROWS, KDIM), BF16), pltpu.VMEM((KDIM, NSEC * ROWS), BF16),
         pltpu.VMEM((KDIM, 128 * max(TILES)), F32),
     ]
     sizes = [128 * t for t in TILES]
@@ -335,7 +381,8 @@
         (lambda n: (ROWS, n), F32), (lambda n: (ROWS, n), BF16), (lambda n: (NSEC * ROWS, n), BF16),
     ):
         buffers += [pltpu.VMEM(shape(n), kind) for n in sizes]
-    sems = [dma((2,)), dma((2,)), dma((2, 4)), dma((2, 4)), dma((2, 2)), dma((2, 2)), dma((5,)), dma((5,)), dma((2, 8)), dma((2, 8)),
+    sems = [dma((4,)), dma((2, 2)), dma((2, 2)), dma((2, 4, 2)), dma((2, 4, 2)), dma((2, 2, 2)), dma((2, 2, 2)), dma((5, 2)), dma((5, 2)),
+            dma((2, 8, 2)), dma((2, 8, 2)),
             dma((NC,)), dma((NC,)), dma((NC, 2)), dma((NC, 2)), dma((NC, 4)), dma((NC, 4)), dma((NC,)), dma((NC,)),
             dma((NC, 7)), dma((NC, 7))]
     hidden, new_gate, new_up = pl.pallas_call(
@@ -345,10 +392,10 @@
             jax.ShapeDtypeStruct((WIDTH, KDIM), BF16),
             jax.ShapeDtypeStruct((WIDTH, KDIM), BF16),
         ),
-        in_specs=[pl.BlockSpec(memory_space=pltpu.SMEM)] + [vmem] * 4,
+        in_specs=[pl.BlockSpec(memory_space=pltpu.SMEM)] + [pl.BlockSpec(memory_space=pl.ANY)] * 4,
         out_specs=(vmem, vmem, vmem),
         scratch_shapes=buffers + sems,
-        compiler_params=pltpu.CompilerParams(collective_id=0, has_side_effects=True, vmem_limit_bytes=44 << 20),
+        compiler_params=pltpu.CompilerParams(collective_id=0, has_side_effects=True, vmem_limit_bytes=56 << 20),
         cost_estimate=pl.CostEstimate(flops=7516192768, bytes_accessed=8 << 20, transcendentals=ROWS * WIDTH),
         name="projection_pair",
     )(lengths, states, gate_weight, up_weight, upstream.T)

time: 144 us -> 140 us (0.972); the launches traced: 143 us -> 137 us
  Pallas kernels: 135 us -> 132 us
  local copies, waits for them, and re-layouts: 7.38 us -> 4.81 us
    pallas_call x1, Pallas kernels: 135 us -> 132 us  [shards(): pl.pallas_call(kernel, out_shape=(jax.ShapeDtypeStruct((WIDTH, ROWS), BF1...]
    unnamed x13 -> x5, local copies, waits for them, and re-layouts: 7.38 us -> 4.81 us
where the time goes in v5:
time: 140 us; the launch traced here: 137 us
  Pallas kernels  132 us (94%)
  local copies, waits for them, and re-layouts  4.81 us (3%)
    pallas_call x1, Pallas kernels, shards(): pl.pallas_call(kernel, out_shape=(jax.ShapeDtypeStruct((WIDTH, ROWS), BF1...  132 us
    unnamed x5, local copies, waits for them, and re-layouts  4.81 us

profile of v5, /device:TPU:36, one launch (start us, length us, event | category | flops | bytes accessed | tf_op | source)
XLA Modules:
  0.0 137.5 jit_solution(13944131349257138413)
XLA Ops:
  0.6 132.0 %projection_pair.1 = (bf16[448,256]{1,0:T(8,128)(2,1)}, bf16[448,1024]{1,0:T(8,128)(2,1)}, bf16[448,1024]{1,0:T(8,128)(2,1)}) custom-call(s32[8]{0:T(128)} %lengths_ref.1, bf16[256,256]{1,0:T(8,128)(2,1)} %states_hbm.1, bf16[32,14336]{1,0:T(8,128)(2,1)} %gate_hbm.1, bf16[32,14336]{1,0:T(8,128)(2,1)} %up_hbm.1, bf16[448,256]{1,0:T(8,128)(2,1)} %bitcast.7), custom_call_target="tpu_custom_call" | custom-call | flops 7516192768 | bytes 8388608 | tf_op jit(solution)/shard_map/projection_pair/pallas_call | solution.py:388
  132.6 1.6 %copy.11 = bf16[256,448]{0,1:T(8,128)(2,1)} copy(bf16[256,448]{0,1:T(8,128)(2,1)} %bitcast.6) | data formatting | bytes 458752
  134.3 0.0 copy-start
  134.3 2.2 %copy.12 = bf16[1024,448]{0,1:T(8,128)(2,1)} copy(bf16[1024,448]{0,1:T(8,128)(2,1)} %bitcast.5) | data formatting | bytes 1835008
  136.5 0.0 copy-done
  136.5 0.9 copy.13
Async XLA Ops:
  134.3 2.2 %copy-start = (bf16[448,1024]{1,0:T(8,128)(2,1)S(1)}, bf16[448,1024]{1,0:T(8,128)(2,1)}, u32[]{:S(2)}) copy-start(bf16[448,1024]{1,0:T(8,128)(2,1)} %get-tuple-element.8) | copy-start | bytes 2752516

commit v6 on v5

--- a/solution.py
+++ b/solution.py
@@ -50,16 +50,7 @@
     up_dev, down_dev, xl_dev = (sid(xl, yp), shard), (sid(xl, ym), shard), (sid(xo, y), shard)
     zp_dev, zm_dev = (sec, shid(zp, xh, core)), (sec, shid(zm, xh, core))
     core_dev, xh_dev = (sec, shid(z, xh, 1 - core)), (sec, shid(z, 1 - xh, core))
-
-    def crossed(z_):
-        out = 0
-        for bit in (1, 2, 4):
-            one, two = lax.rem(lax.div(z_, bit), 2), lax.rem(lax.div(sec, bit), 2)
-            out = out + bit * (one + two - 2 * one * two)
-        return out
-
-    goal = crossed(z)
-    mid_dev = (sec, shid(goal, xh, core))
+    mid_dev, goal = (sec, shid(lax.rem(z + sec, NZ), xh, core)), lax.rem(z - sec + NZ, NZ)
 
     barrier = pltpu.get_barrier_semaphore()
 
@@ -159,7 +150,7 @@
         return s_buf.at[pl.ds(pl.multiple_of(start, HALF), HALF), cols_of(qq)]
 
     def piece(i, h, qq):
-        return half_of(crossed(lax.rem(z + OFFSETS[i] + NZ, NZ)), h, qq)
+        return half_of(lax.rem(goal + OFFSETS[i] + NZ, NZ), h, qq)
 
     partner = (1 - xh) * 2 + core
     z_devs = (zp_dev, zm_dev)

time: 140 us -> 139 us (level)
  no operation moved by 1% of the time
where the time goes in v6:
time: 139 us; the launch traced here: 136 us
  Pallas kernels  131 us (94%)
  local copies, waits for them, and re-layouts  4.81 us (3%)
    pallas_call x1, Pallas kernels, shards(): pl.pallas_call(kernel, out_shape=(jax.ShapeDtypeStruct((WIDTH, ROWS), BF1...  131 us
    unnamed x5, local copies, waits for them, and re-layouts  4.81 us

profile of v6, /device:TPU:36, one launch (start us, length us, event | category | flops | bytes accessed | tf_op | source)
XLA Modules:
  0.0 136.3 jit_solution(8312807372170225140)
XLA Ops:
  0.6 130.9 %projection_pair.1 = (bf16[448,256]{1,0:T(8,128)(2,1)}, bf16[448,1024]{1,0:T(8,128)(2,1)}, bf16[448,1024]{1,0:T(8,128)(2,1)}) custom-call(s32[8]{0:T(128)} %lengths_ref.1, bf16[256,256]{1,0:T(8,128)(2,1)} %states_hbm.1, bf16[32,14336]{1,0:T(8,128)(2,1)} %gate_hbm.1, bf16[32,14336]{1,0:T(8,128)(2,1)} %up_hbm.1, bf16[448,256]{1,0:T(8,128)(2,1)} %bitcast.7), custom_call_target="tpu_custom_call" | custom-call | flops 7516192768 | bytes 8388608 | tf_op jit(solution)/shard_map/projection_pair/pallas_call | solution.py:379
  131.5 1.6 %copy.11 = bf16[256,448]{0,1:T(8,128)(2,1)} copy(bf16[256,448]{0,1:T(8,128)(2,1)} %bitcast.6) | data formatting | bytes 458752
  133.2 0.0 copy-start
  133.2 2.2 %copy.12 = bf16[1024,448]{0,1:T(8,128)(2,1)} copy(bf16[1024,448]{0,1:T(8,128)(2,1)} %bitcast.5) | data formatting | bytes 1835008
  135.4 0.0 copy-done
  135.4 0.9 copy.13
Async XLA Ops:
  133.2 2.2 %copy-start = (bf16[448,1024]{1,0:T(8,128)(2,1)S(1)}, bf16[448,1024]{1,0:T(8,128)(2,1)}, u32[]{:S(2)}) copy-start(bf16[448,1024]{1,0:T(8,128)(2,1)} %get-tuple-element.8) | copy-start | bytes 2752516
